TPU v7x, 32 devices: a whole 2x2x4 slice. The times are simulated.
32 devices in a mesh: row: 8 (over z, core), col: 4 (over y, x).
Axes of the slice: x: 2, y: 2, z: 4, core: 2. Of those that a mesh axis runs over, the one named last changes fastest.
Arguments:
- eigvecs: float32 [512, 262144], P(('row', 'col')), may hold values from -6 to 6
- panels: bfloat16 [4, 262144, 128], P('col', 'row'), may hold values from -0.01171875 to 0.01171875
- tfactors: bfloat16 [4, 128, 128], P('col'), as said below
- owners: int32 [4], replicated, may hold values from 0 to 3, as said below
- offsets: int32 [4], replicated, may hold values from 0 to 65408, as said below
Outputs:
- back: float32 [512, 262144], P('col', 'row')
Inputs may be any that keep to these rules, and one draw needn't show every extreme that they name: `owners`: distinct grid columns. `offsets`: multiples of 128. `tfactors`: each matrix is upper triangular with its diagonal between 1 and 8.
All inputs are finite; a program needn't handle non-finite values.
Results may differ from a plain program's by a relative error of at most 0.0003.
Values may be sent and summed in bfloat16 or wider, within the bound.
A program may use at most 192 MiB of HBM per device.

v0:
```python
import jax
import jax.numpy as jnp
from jax import lax
from jax.sharding import PartitionSpec as P

PANELS = 4


def from_root(value, axis, root):
    mine = lax.axis_index(axis) == root
    return lax.psum(jnp.where(mine, value, jnp.zeros_like(value)), axis)


def reflector_block(stored, offset, first_row):
    row_ids = first_row + lax.broadcasted_iota(jnp.int32, stored.shape, 0)
    col_ids = lax.broadcasted_iota(jnp.int32, stored.shape, 1)
    below = row_ids - col_ids - offset
    unit = jnp.where(below == 0, jnp.float32(1.0), jnp.float32(0.0))
    return jnp.where(below > 0, stored.astype(jnp.float32), unit)


def local(eigvecs, panels, tfactors, owners, offsets):
    highest = lax.Precision.HIGHEST
    spread = lax.all_to_all(eigvecs, ("row", "col"), split_axis=1, concat_axis=0, tiled=True)
    field = lax.all_to_all(spread, "col", split_axis=0, concat_axis=1, tiled=True)
    local_rows = field.shape[1]
    first_row = lax.axis_index("row") * local_rows
    for panel in reversed(range(PANELS)):
        stored, triangle = (
            from_root(panels[0], "col", owners[panel]),
            from_root(tfactors[0], "col", owners[panel]),
        )
        reflector = reflector_block(stored, offsets[panel], first_row)
        partial_sum = jnp.dot(
            field, reflector, precision=highest, preferred_element_type=jnp.float32
        )
        projection = lax.psum(partial_sum, "row")
        coeffs = jnp.dot(
            projection,
            triangle.astype(jnp.float32).T,
            precision=highest,
            preferred_element_type=jnp.float32,
        )
        field = field - jnp.dot(
            coeffs, reflector.T, precision=highest, preferred_element_type=jnp.float32
        )
    return field


def solution(mesh):
    in_specs = (P(("row", "col"), None), P("col", "row", None), P("col", None, None), P(), P())
    out_specs = P("col", "row")
    return jax.shard_map(local, mesh=mesh, in_specs=in_specs, out_specs=out_specs, check_vma=False)
```

profile of v0, /device:TPU:0, one launch (start us, length us, event | category | flops | bytes accessed | tf_op | source)
XLA Modules:
  0.0 1452.2 jit_solution(3471841519852372814)
XLA Ops:
  6.5 11.7 copy.14
  18.2 0.0 copy-start.8
  18.2 7.4 all-to-all-start
  25.6 0.0 all-reduce.19.cloned.1.call-start
  25.7 0.0 copy-done.8
  25.7 0.6 fusion.82
  28.8 13.5 select_bitcast_fusion
  42.3 0.0 all-reduce.19.cloned.1.call-update
  42.3 365.0 %all-to-all-done = f32[16,32,8192]{2,0,1:T(8,128)} async-done(((f32[16,32,8192]{2,0,1:T(8,128)}), f32[16,32,8192]{2,0,1:T(8,128)}, u32[]{:S(2)}, u32[]{:S(2)}) %all-to-all-start) | async-done | bytes 16777248 | tf_op jit(solution)/shard_map/all_to_all | solution.py:24
  407.4 0.0 copy-start.7
  407.4 0.0 copy-start.9
  407.4 8.2 all-to-all-start.1
  415.6 0.0 all-reduce.17.cloned.1.call-start
  415.7 0.0 copy-done.7
  415.7 0.7 select_bitcast_fusion.4
  416.3 0.0 all-reduce.17.cloned.1.call-update
  416.4 0.0 all-reduce.9.cloned.1.call-start
  416.4 0.0 copy-done.9
  416.4 0.6 fusion.81
  417.0 265.8 %all-to-all-done.1 = f32[4,128,8192]{2,1,0:T(8,128)} async-done(((f32[4,128,8192]{2,1,0:T(8,128)}), f32[4,128,8192]{2,1,0:T(8,128)}, u32[]{:S(2)}, u32[]{:S(2)}) %all-to-all-start.1) | async-done | bytes 16777248 | tf_op jit(solution)/shard_map/all_to_all | solution.py:25
  682.9 12.2 copy.12
  695.0 280.7 %all-reduce.19.cloned.1.call-done = (bf16[32768,128]{1,0:T(8,128)(2,1)}, bf16[32768,128]{1,0:T(8,128)(2,1)}, bf16[32768,128]{1,0:T(8,128)(2,1)}, bf16[32768,128]{1,0:T(8,128)(2,1)}) async-done(((bf16[32768,128]{1,0:T(8,128)(2,1)}, bf16[32768,128]{1,0:T(8,128)(2,1)}, bf16[32768,128]{1,0:T(8,128)(2,1)}, bf16[32768,128]{1,0:T(8,128)(2,1)}), (bf16[32768,128]{1,0:T(8,128)(2,1)}, bf16[32768,128]{1,0:T(8,128)(2,1)}, ...) | async-done | bytes 33554448 | tf_op jit(solution)/shard_map/psum | solution.py:11
  975.7 31.7 %fusion.56 = f32[128,128]{0,1:T(8,128)} fusion(f32[128,32768]{1,0:T(8,128)} %bitcast.55, bf16[32768,128]{1,0:T(8,128)(2,1)} %get-tuple-element.9, s32[]{:T(128)} %bitcast.3, s32[32768]{0:T(1024)S(1)} %iota_add_fusion), kind=kOutput, calls=%fused_computation.70 | convolution fusion | flops 6471811072 | bytes 25362436 | tf_op jit(solution)/shard_map/dot_general | solution.py:34
  1007.4 0.0 all-reduce.9.cloned.1.call-update
  1007.5 0.0 all-reduce.11.cloned.1.call-start
  1007.5 14.8 %all-reduce.17.cloned.1.call-done = (bf16[128,128]{1,0:T(8,128)(2,1)}, bf16[128,128]{1,0:T(8,128)(2,1)}, bf16[128,128]{1,0:T(8,128)(2,1)}, bf16[128,128]{1,0:T(8,128)(2,1)}) async-done(((bf16[128,128]{1,0:T(8,128)(2,1)}, bf16[128,128]{1,0:T(8,128)(2,1)}, bf16[128,128]{1,0:T(8,128)(2,1)}, bf16[128,128]{1,0:T(8,128)(2,1)}), (bf16[128,128]{1,0:T(8,128)(2,1)}, bf16[128,128]{1,0:T(8,128)(2,1)}, ...) | async-done | bytes 131088 | tf_op jit(solution)/shard_map/psum | solution.py:11
  1022.3 56.0 %all-reduce.9.cloned.1.call-done = f32[128,128]{0,1:T(8,128)} async-done(((f32[128,128]{0,1:T(8,128)}), f32[128,128]{0,1:T(8,128)}) %all-reduce.9.cloned.1.call-update) | async-done | bytes 65552 | tf_op jit(solution)/shard_map/psum | solution.py:37
  1078.3 1.1 fusion.83
  1079.4 0.0 copy-start.3
  1079.4 21.6 %convolution_subtract_fusion.3 = f32[128,32768]{1,0:T(8,128)S(1)} fusion(f32[128,32768]{1,0:T(8,128)} %bitcast.56, f32[128,128]{1,0:T(8,128)S(1)} %fusion.83, bf16[32768,128]{1,0:T(8,128)(2,1)} %get-tuple-element.9, s32[]{:T(128)} %bitcast.3, s32[32768]{0:T(1024)S(1)} %iota_add_fusion), kind=kOutput, calls=%fused_computation.3 | convolution fusion | flops 6476005376 | bytes 42139652 | tf_op jit(solution)/shard_map/dot_general | solution.py:44
  1101.0 0.0 copy-start.1
  1101.0 6.2 copy-done.1
  1107.1 0.0 copy-done.3
  1107.1 0.0 copy-start.6
  1107.1 41.6 %fusion.13 = f32[128,128]{1,0:T(8,128)} fusion(f32[128,32768]{1,0:T(8,128)S(1)} %convolution_subtract_fusion.3, bf16[32768,128]{1,0:T(8,128)(2,1)S(1)} %copy-done.3, s32[]{:T(128)} %bitcast.8, s32[32768]{0:T(1024)S(1)} %iota_add_fusion), kind=kOutput, calls=%fused_computation.23 | convolution fusion | flops 6471811072 | bytes 25362436 | tf_op jit(solution)/shard_map/dot_general | solution.py:34
  1148.7 0.0 all-reduce.11.cloned.1.call-update
  1148.8 0.0 all-reduce.13.cloned.1.call-start
  1148.8 52.7 %all-reduce.11.cloned.1.call-done = f32[128,128]{1,0:T(8,128)} async-done(((f32[128,128]{1,0:T(8,128)}), f32[128,128]{1,0:T(8,128)}) %all-reduce.11.cloned.1.call-update) | async-done | bytes 65552 | tf_op jit(solution)/shard_map/psum | solution.py:37
  1201.5 0.0 copy-done.6
  1201.5 1.0 fusion.84
  1202.6 21.3 %convolution_subtract_fusion.2 = f32[128,32768]{1,0:T(8,128)S(1)} fusion(f32[128,32768]{1,0:T(8,128)} %copy-done.1, f32[128,128]{1,0:T(8,128)S(1)} %fusion.84, bf16[32768,128]{1,0:T(8,128)(2,1)} %get-tuple-element.10, s32[]{:T(128)} %bitcast.8, s32[32768]{0:T(1024)S(1)} %iota_add_fusion), kind=kOutput, calls=%fused_computation.2 | convolution fusion | flops 6476005376 | bytes 42139652 | tf_op jit(solution)/shard_map/dot_general | solution.py:44
  1223.9 0.0 copy-start.2
  1223.9 6.2 copy-done.2
  1230.0 0.0 copy-start.5
  1230.0 28.8 %fusion.14 = f32[128,128]{1,0:T(8,128)} fusion(f32[128,32768]{1,0:T(8,128)S(1)} %convolution_subtract_fusion.2, bf16[32768,128]{1,0:T(8,128)(2,1)} %get-tuple-element.11, s32[]{:T(128)} %bitcast.12, s32[32768]{0:T(1024)S(1)} %iota_add_fusion), kind=kOutput, calls=%fused_computation.24 | convolution fusion | flops 6471811072 | bytes 25362436 | tf_op jit(solution)/shard_map/dot_general | solution.py:34
  1258.8 0.0 all-reduce.13.cloned.1.call-update
  1258.8 0.2 all-reduce.15.cloned.1.call-start
  1259.0 52.6 %all-reduce.13.cloned.1.call-done = f32[128,128]{1,0:T(8,128)} async-done(((f32[128,128]{1,0:T(8,128)}), f32[128,128]{1,0:T(8,128)}) %all-reduce.13.cloned.1.call-update) | async-done | bytes 65552 | tf_op jit(solution)/shard_map/psum | solution.py:37
  1311.6 0.0 copy-done.5
  1311.6 1.0 fusion.85
  1312.7 21.3 %convolution_subtract_fusion.1 = f32[128,32768]{1,0:T(8,128)S(1)} fusion(f32[128,32768]{1,0:T(8,128)} %copy-done.2, f32[128,128]{1,0:T(8,128)S(1)} %fusion.85, bf16[32768,128]{1,0:T(8,128)(2,1)} %get-tuple-element.11, s32[]{:T(128)} %bitcast.12, s32[32768]{0:T(1024)S(1)} %iota_add_fusion), kind=kOutput, calls=%fused_computation.1 | convolution fusion | flops 6476005376 | bytes 42139652 | tf_op jit(solution)/shard_map/dot_general | solution.py:44
  1333.9 0.0 copy-start
  1333.9 6.2 copy-done
  1340.1 0.0 copy-start.4
  1340.1 28.8 %fusion.15 = f32[128,128]{1,0:T(8,128)} fusion(f32[128,32768]{1,0:T(8,128)S(1)} %convolution_subtract_fusion.1, bf16[32768,128]{1,0:T(8,128)(2,1)} %get-tuple-element.12, s32[]{:T(128)} %bitcast.16, s32[32768]{0:T(1024)S(1)} %iota_add_fusion), kind=kOutput, calls=%fused_computation.25 | convolution fusion | flops 6471811072 | bytes 25362436 | tf_op jit(solution)/shard_map/dot_general | solution.py:34
  1368.9 0.0 all-reduce.15.cloned.1.call-update
  1368.9 52.8 %all-reduce.15.cloned.1.call-done = f32[128,128]{1,0:T(8,128)} async-done(((f32[128,128]{1,0:T(8,128)}), f32[128,128]{1,0:T(8,128)}) %all-reduce.15.cloned.1.call-update) | async-done | bytes 65552 | tf_op jit(solution)/shard_map/psum | solution.py:37
  1421.7 0.0 copy-done.4
  1421.7 1.0 fusion.86
  1422.7 22.7 %convolution_subtract_fusion = f32[128,32768]{1,0:T(8,128)} fusion(f32[128,32768]{1,0:T(8,128)} %copy-done, f32[128,128]{1,0:T(8,128)S(1)} %fusion.86, bf16[32768,128]{1,0:T(8,128)(2,1)} %get-tuple-element.12, s32[]{:T(128)} %bitcast.16, s32[32768]{0:T(1024)S(1)} %iota_add_fusion), kind=kOutput, calls=%fused_computation | convolution fusion | flops 6476005376 | bytes 42139652 | tf_op jit(solution)/shard_map/dot_general | solution.py:44
  (1 shorter events, 0.0 us)
Async XLA Ops:
  18.2 7.5 copy-start.8
  18.2 389.2 %all-to-all-start = ((f32[16,32,8192]{2,0,1:T(8,128)}), f32[16,32,8192]{2,0,1:T(8,128)}, u32[]{:S(2)}, u32[]{:S(2)}) async-start(f32[16,32,8192]{2,0,1:T(8,128)} %bitcast.57), calls=%async_computation | async-start | bytes 33554432 | tf_op jit(solution)/shard_map/all_to_all | solution.py:24
  25.6 950.1 %all-reduce.19.cloned.1.call-start = ((), (), s32[]{:S(2)}) async-start(), calls=%async_computation.7 | async-start | bytes 67108864 | tf_op jit(solution)/shard_map/psum | solution.py:11
  407.4 8.3 copy-start.7
  407.4 9.0 copy-start.9
  407.4 275.5 %all-to-all-start.1 = ((f32[4,128,8192]{2,1,0:T(8,128)}), f32[4,128,8192]{2,1,0:T(8,128)}, u32[]{:S(2)}, u32[]{:S(2)}) async-start(f32[4,128,8192]{2,1,0:T(8,128)} %bitcast.1), calls=%async_computation.1 | async-start | bytes 33554432 | tf_op jit(solution)/shard_map/all_to_all | solution.py:25
  415.6 606.7 %all-reduce.17.cloned.1.call-start = ((), (), s32[]{:S(2)}) async-start(), calls=%async_computation.6 | async-start | bytes 262144 | tf_op jit(solution)/shard_map/psum | solution.py:11
  416.4 661.9 %all-reduce.9.cloned.1.call-start = ((), (), s32[]{:S(2)}) async-start(), calls=%async_computation.2 | async-start | bytes 131072 | tf_op jit(solution)/shard_map/psum | solution.py:37
  1007.5 194.0 %all-reduce.11.cloned.1.call-start = ((), (), s32[]{:S(2)}) async-start(), calls=%async_computation.3 | async-start | bytes 131072 | tf_op jit(solution)/shard_map/psum | solution.py:37
  1079.4 27.7 %copy-start.3 = (bf16[32768,128]{1,0:T(8,128)(2,1)S(1)}, bf16[32768,128]{1,0:T(8,128)(2,1)}, u32[]{:S(2)}) copy-start(bf16[32768,128]{1,0:T(8,128)(2,1)} %get-tuple-element.10) | copy-start | bytes 25165828
  1101.0 6.2 copy-start.1
  1107.1 94.4 %copy-start.6 = (bf16[128,128]{1,0:T(8,128)(2,1)S(1)}, bf16[128,128]{1,0:T(8,128)(2,1)}, u32[]{:S(2)}) copy-start(bf16[128,128]{1,0:T(8,128)(2,1)} %get-tuple-element.6) | copy-start | bytes 98308
  1148.8 162.9 %all-reduce.13.cloned.1.call-start = ((), (), s32[]{:S(2)}) async-start(), calls=%async_computation.4 | async-start | bytes 131072 | tf_op jit(solution)/shard_map/psum | solution.py:37
  1223.9 6.2 copy-start.2
  1230.0 81.6 %copy-start.5 = (bf16[128,128]{1,0:T(8,128)(2,1)S(1)}, bf16[128,128]{1,0:T(8,128)(2,1)}, u32[]{:S(2)}) copy-start(bf16[128,128]{1,0:T(8,128)(2,1)} %get-tuple-element.7) | copy-start | bytes 98308
  1258.8 162.9 %all-reduce.15.cloned.1.call-start = ((), (), s32[]{:S(2)}) async-start(), calls=%async_computation.5 | async-start | bytes 131072 | tf_op jit(solution)/shard_map/psum | solution.py:37
  1333.9 6.2 copy-start
  1340.1 81.6 %copy-start.4 = (bf16[128,128]{1,0:T(8,128)(2,1)S(1)}, bf16[128,128]{1,0:T(8,128)(2,1)}, u32[]{:S(2)}) copy-start(bf16[128,128]{1,0:T(8,128)(2,1)} %get-tuple-element.8) | copy-start | bytes 98308
Sparse Core Ops, SparseCore 0:
  42.5 933.2 all-reduce.18
  979.0 43.2 all-reduce.16
  1024.6 53.5 all-reduce.8
  1148.9 52.5 all-reduce.10
  1258.9 52.6 all-reduce.12
  1369.1 52.5 all-reduce.14
where the time goes:
time: 1450 us
  waiting for transfers between devices  1140 us (79%)
  matrix products  222 us (15%)
  local copies, waits for them, and re-layouts  43.6 us (3%)
  starting transfers between devices  16.1 us (1%)
  between operations  16.1 us (1%)
    all_to_all x1, waiting for transfers between devices, local(): lax.all_to_all(eigvecs, ('row', 'col'), split_axis=1, concat_axis=0, tile...  365 us
    psum x2, waiting for transfers between devices, from_root(): return lax.psum(jnp.where(mine, value, jnp.zeros_like(value)), axis)  295 us
    all_to_all x1, waiting for transfers between devices, local(): lax.all_to_all(spread, 'col', split_axis=0, concat_axis=1, tiled=True)  266 us
    psum x4, waiting for transfers between devices, local(): projection = lax.psum(partial_sum, 'row')  214 us
    dot_general x4, matrix products, local(): jnp.dot(field, reflector, precision=highest, preferred_element_type=jnp.f...  131 us
    dot_general x4, matrix products, local(): jnp.dot(coeffs, reflector.T, precision=highest, preferred_element_type=jn...  86.8 us
  transfers between devices with their start and end apart: 8, of which 8 were waited for; matrix products, arithmetic and copies ran while one was open for 4% of the time, Pallas kernels for 0%

commit v1 on v0

v1 whole, which is shorter than its diff:
```python
import jax
import jax.numpy as jnp
from jax import lax
from jax.sharding import PartitionSpec as P

PANELS = 4
GROUP = 128
TOP = 32767.0


def encode(value):
    rows, columns = value.shape
    grouped = value.reshape(rows, columns // GROUP, GROUP)
    peak = jnp.max(jnp.abs(grouped), axis=2)
    peak = jnp.maximum(peak, jnp.float32(1e-30))
    code = jnp.round(grouped * (TOP / peak)[:, :, None])
    code = jnp.clip(code, -TOP, TOP).astype(jnp.int16)
    return code.reshape(rows, columns), peak * jnp.float32(1.0 / TOP)


def decode(code, step):
    rows, columns = code.shape
    grouped = code.reshape(rows, columns // GROUP, GROUP).astype(jnp.float32)
    return (grouped * step[:, :, None]).reshape(rows, columns)


def split(value):
    high = lax.reduce_precision(value, 8, 7)
    return high.astype(jnp.bfloat16), (value - high).astype(jnp.bfloat16)


def reflector_block(stored, offset, first_row):
    row_ids = first_row + lax.broadcasted_iota(jnp.int32, stored.shape, 0)
    col_ids = lax.broadcasted_iota(jnp.int32, stored.shape, 1)
    below = row_ids - col_ids - offset
    unit = jnp.where(below == 0, jnp.bfloat16(1.0), jnp.bfloat16(0.0))
    return jnp.where(below > 0, stored, unit)


def dot(a, b, contract):
    return lax.dot_general(a, b, (contract, ((), ())), preferred_element_type=jnp.float32)


def local(eigvecs, panels, tfactors, owners, offsets):
    highest = lax.Precision.HIGHEST
    both = ("row", "col")
    n_col = lax.axis_size("col")
    stored = lax.all_to_all(panels[0], "col", split_axis=0, concat_axis=0, tiled=True)
    triangles = lax.all_gather(tfactors[0], "col")
    code, step = encode(eigvecs)
    code = lax.all_to_all(code, both, split_axis=1, concat_axis=0, tiled=True)
    step = lax.all_to_all(step, both, split_axis=1, concat_axis=0, tiled=True)
    local_rows = code.shape[1]
    first_row = (lax.axis_index("row") * n_col + lax.axis_index("col")) * local_rows
    stored = stored.reshape(n_col, local_rows, stored.shape[-1])
    reflectors = [
        reflector_block(
            lax.dynamic_index_in_dim(stored, owners[panel], 0, keepdims=False),
            offsets[panel],
            first_row,
        )
        for panel in range(PANELS)
    ]
    reflector = jnp.concatenate(reflectors, axis=1)
    nb = reflector.shape[1] // PANELS
    gram = lax.psum(dot(reflector, reflector, ((0,), (0,))), both)
    field = decode(code, step)
    high, low = split(field)
    product = dot(high, reflector, ((1,), (0,))) + dot(low, reflector, ((1,), (0,)))
    projection = lax.psum(product, both)
    coeffs = [None] * PANELS
    for panel in reversed(range(PANELS)):
        at = slice(panel * nb, (panel + 1) * nb)
        inner = projection[:, at]
        for later in range(panel + 1, PANELS):
            block = gram[later * nb : (later + 1) * nb, at]
            inner = inner - jnp.dot(coeffs[later], block, precision=highest)
        triangle = lax.dynamic_index_in_dim(triangles, owners[panel], 0, keepdims=False)
        coeffs[panel] = jnp.dot(inner, triangle.astype(jnp.float32).T, precision=highest)
    high, low = split(jnp.concatenate(coeffs, axis=1))
    change = dot(high, reflector, ((1,), (1,))) + dot(low, reflector, ((1,), (1,)))
    code, step = encode(field - change)
    code = lax.all_to_all(code, "col", split_axis=0, concat_axis=1, tiled=True)
    step = lax.all_to_all(step, "col", split_axis=0, concat_axis=1, tiled=True)
    return decode(code, step)


def solution(mesh):
    in_specs = (P(("row", "col"), None), P("col", "row", None), P("col", None, None), P(), P())
    out_specs = P("col", "row")
    return jax.shard_map(local, mesh=mesh, in_specs=in_specs, out_specs=out_specs, check_vma=False)
```

time: 1450 us -> 770 us (0.53)
  waiting for transfers between devices: 1140 us -> 433 us
  matrix products: 222 us -> 65.6 us
  other arithmetic: 14.2 us -> 130 us
  local copies, waits for them, and re-layouts: 43.6 us -> 69.9 us
  blocking collectives: 0 us -> 22.8 us
    psum x6 -> x1, waiting for transfers between devices: 509 us -> 128 us  [local(): projection = lax.psum(product, both)]
    all_to_all x2 -> x4, waiting for transfers between devices: 631 us -> 305 us  [the longest x1 159 us: local(): code = lax.all_to_all(code, both, split_axis=1, concat_axis=0, tiled=True)]
    dot_general x12 -> x15, matrix products: 222 us -> 65.6 us  [the longest x5 54.4 us: dot(): lax.dot_general(a, b, (contract, ((), ())), preferred_element_type=jnp.fl...]
    convert_element_type x0 -> x2, other arithmetic: none -> 41.6 us  [encode(): code = jnp.clip(code, -TOP, TOP).astype(jnp.int16)]
    mul x0 -> x3, other arithmetic: none -> 37.5 us  [the longest x2 37.5 us: decode(): return (grouped * step[:, :, None]).reshape(rows, columns)]
    mul x0 -> x8, local copies, waits for them, and re-layouts: none -> 25.7 us  [the longest x3 15.5 us: decode(): return (grouped * step[:, :, None]).reshape(rows, columns)]
    unnamed x0 -> x3, other arithmetic: none -> 25.6 us
    all_to_all x2, local copies, waits for them, and re-layouts: 23.8 us -> 8.13 us  [the longest x1 7.61 us: local(): code = lax.all_to_all(code, both, split_axis=1, concat_axis=0, tiled=True)]
  transfers between devices with their start and end apart: 8 -> 5, of which waited for: 8 -> 4; matrix products, arithmetic and copies ran while one was open for 4% -> 10% of each run, Pallas kernels for 0% -> 0%
where the time goes in v1:
time: 770 us; the launch traced here: 762 us
  waiting for transfers between devices  433 us (56%)
  other arithmetic  130 us (17%)
  local copies, waits for them, and re-layouts  69.9 us (9%)
  matrix products  65.6 us (9%)
  blocking collectives  22.8 us (3%)
  between operations  21.4 us (3%)
  starting transfers between devices  19.3 us (3%)
    all_to_all x1, waiting for transfers between devices, local(): code = lax.all_to_all(code, both, split_axis=1, concat_axis=0, tiled=True)  159 us
    psum x1, waiting for transfers between devices, local(): projection = lax.psum(product, both)  128 us
    all_to_all x1, waiting for transfers between devices, local(): code = lax.all_to_all(code, 'col', split_axis=0, concat_axis=1, tiled=True)  91.4 us
    dot_general x5, matrix products, dot(): lax.dot_general(a, b, (contract, ((), ())), preferred_element_type=jnp.fl...  54.4 us
    all_to_all x1, waiting for transfers between devices, local(): lax.all_to_all(panels[0], 'col', split_axis=0, concat_axis=0, tiled=True)  54.2 us
    convert_element_type x2, other arithmetic, encode(): code = jnp.clip(code, -TOP, TOP).astype(jnp.int16)  41.6 us
    mul x2, other arithmetic, decode(): return (grouped * step[:, :, None]).reshape(rows, columns)  37.5 us
    unnamed x22, local copies, waits for them, and re-layouts  28.1 us
  transfers between devices with their start and end apart: 5, of which 4 were waited for; matrix products, arithmetic and copies ran while one was open for 10% of the time, Pallas kernels for 0%

profile of v1, /device:TPU:0, one launch (start us, length us, event | category | flops | bytes accessed | tf_op | source)
XLA Modules:
  0.0 761.6 jit_solution(6139125567761827339)
XLA Ops:
  6.5 6.6 abs_bitcast_fusion.1
  13.2 12.3 %copy.30 = f32[2,8,2048,128]{3,2,1,0:T(8,128)S(1)} copy(f32[2,8,2048,128]{3,1,2,0:T(8,128)S(1)} %abs_bitcast_fusion.1) | data formatting | bytes 33554432
  25.5 5.8 bitcast_reduce_fusion
  31.3 0.1 mul.79
  31.4 0.2 copy.43
  31.6 0.2 reshape.65
  31.8 15.5 %all_to_all.61 = f32[32,1,1024]{2,1,0:T(1,128)S(1)} all-to-all(f32[32,1,1024]{2,1,0:T(1,128)S(1)} %reshape.65), channel_id=1, replica_groups=mesh['row'=8,'col'=4] {'row','col'}, dimensions={0} | all-to-all | bytes 262144 | tf_op jit(solution)/shard_map/all_to_all | solution.py:52
  47.3 5.6 all-to-all-start.2
  52.9 4.6 mul.74
  57.5 25.6 %fusion.6 = s16[16,262144]{1,0:T(8,128)(2,1)} fusion(f32[16,262144]{1,0:T(8,128)} %param.5, f32[2,8,2048,128]{3,2,1,0:T(8,128)S(1)} %bitcast.98), kind=kLoop, calls=%fused_computation.12 | loop fusion | flops 16777216 | bytes 41943040 | tf_op jit(solution)/shard_map/convert_element_type | solution.py:17
  83.1 7.6 copy.42
  90.7 54.2 %all-to-all-done.2 = bf16[4,8192,128]{2,1,0:T(8,128)(2,1)} async-done(((bf16[4,8192,128]{2,1,0:T(8,128)(2,1)}), bf16[4,8192,128]{2,1,0:T(8,128)(2,1)}, u32[]{:S(2)}, u32[]{:S(2)}) %all-to-all-start.2) | async-done | bytes 8388640 | tf_op jit(solution)/shard_map/all_to_all | solution.py:48
  144.9 3.8 all-to-all-start
  148.7 0.5 all-reduce.3.cloned.1.call-start
  149.2 0.0 copy-done.7
  149.2 0.6 fusion.61
  157.1 0.6 fusion.60
  157.7 0.5 broadcast.46
  158.2 0.9 reduce
  159.2 0.1 reshape.66
  159.3 10.2 %fusion.28 = (bf16[8192,128]{1,0:T(8,128)(2,1)S(1)}, bf16[8192,128]{1,0:T(8,128)(2,1)S(1)}, bf16[8192,128]{1,0:T(8,128)(2,1)S(1)}, bf16[8192,128]{1,0:T(8,128)(2,1)S(1)}) fusion(bf16[4,8192,128]{2,1,0:T(8,128)(2,1)} %all-to-all-done.2, s32[]{:T(128)S(6)} %select_n.44, s32[]{:T(128)} %bitcast.4, s32[8192]{0:T(1024)S(1)} %iota_add_fusion, s32[]{:T(128)S(6)} %select_n.53, ...), kind=kLoop, calls=%fused_computation.41 | loop fusion | flops 22020096 | bytes 16810016 | tf_op jit(solution)/shard_map/jit(_where)/select_n | solution.py:37
  169.6 1.3 copy-done.1
  170.9 0.6 copy-done.4
  171.5 0.7 copy-done.5
  172.2 5.5 fusion.59
  177.7 159.3 %all-to-all-done = s16[16,32,8192]{2,0,1:T(8,128)(2,1)} async-done(((s16[16,32,8192]{2,0,1:T(8,128)(2,1)}), s16[16,32,8192]{2,0,1:T(8,128)(2,1)}, u32[]{:S(2)}, u32[]{:S(2)}) %all-to-all-start) | async-done | bytes 8388640 | tf_op jit(solution)/shard_map/all_to_all | solution.py:51
  337.0 7.0 mul.81
  343.9 19.3 %bitcast_multiply_fusion.2 = f32[512,8192]{1,0:T(8,128)S(1)} fusion(f32[64,8,64,128]{3,2,1,0:T(8,128)} %bitcast.95, s16[16,32,8192]{2,0,1:T(8,128)(2,1)} %all-to-all-done), kind=kLoop, calls=%fused_computation.8 | loop fusion | flops 8388608 | bytes 41943040 | tf_op jit(solution)/shard_map/mul | solution.py:24
  363.3 0.0 copy-start
  363.3 6.2 copy-done
  369.4 6.8 fusion.7
  376.2 0.0 copy-start.6
  376.2 12.5 %fusion.30 = f32[512,512]{1,0:T(8,128)} fusion(f32[512,512]{1,0:T(8,128)S(1)} %fusion.7, f32[512,8192]{1,0:T(8,128)} %copy-done, bf16[8192,128]{1,0:T(8,128)(2,1)S(1)} %copy-done.2, bf16[8192,128]{1,0:T(8,128)(2,1)} %copy-done.4, bf16[8192,128]{1,0:T(8,128)(2,1)} %copy-done.5, bf16[8192,128]{1,0:T(8,128)(2,1)S(1)} %get-tuple-element.7), kind=kOutput, calls=%fused_computation.45 | convolution fusion | flops 4337172480 | bytes 27262976 | tf_op jit(solution)/shard_map/dot_general | solution.py:41
  388.7 0.0 all-reduce.3.cloned.1.call-update
  388.8 7.3 all_gather.3
  396.1 127.7 %all-reduce.3.cloned.1.call-done = (f32[512,512]{1,0:T(8,128)}, f32[512,512]{1,0:T(8,128)}) async-done(((f32[512,512]{1,0:T(8,128)}, f32[512,512]{1,0:T(8,128)}), (f32[512,512]{1,0:T(8,128)}, f32[512,512]{1,0:T(8,128)})) %all-reduce.3.cloned.1.call-update) | async-done | bytes 2097168 | tf_op jit(solution)/shard_map/psum | solution.py:70
  523.8 1.2 fusion.34
  525.1 1.6 convolution_subtract_fusion.5
  526.6 0.3 fusion.46
  527.0 1.6 convolution_subtract_fusion.4
  528.6 1.4 convolution_subtract_fusion.3
  530.0 0.3 fusion.44
  530.3 1.6 convolution_subtract_fusion.2
  531.9 1.4 convolution_subtract_fusion.1
  533.3 1.4 convolution_subtract_fusion
  534.8 0.3 fusion.42
  535.1 10.3 %fusion.33 = f32[512,8192]{1,0:T(8,128)} fusion(f32[512,128]{0,1:T(8,128)S(1)} %fusion.34, f32[512,128]{0,1:T(8,128)S(1)} %fusion.46, f32[512,128]{0,1:T(8,128)S(1)} %fusion.44, f32[512,128]{0,1:T(8,128)S(1)} %fusion.42, bf16[8192,128]{1,0:T(8,128)(2,1)} %copy-done.1, bf16[8192,128]{1,0:T(8,128)(2,1)} %copy-done.4, bf16[8192,128]{1,0:T(8,128)(2,1)} %copy-done.5, ...), kind=kOutput, calls=%fused_computation.54 | convolution fusion | flops 4329832448 | bytes 26214400 | tf_op jit(solution)/shard_map/dot_general | solution.py:41
  545.4 19.3 %add_subtract_fusion = f32[512,8192]{1,0:T(8,128)} fusion(f32[512,8192]{1,0:T(8,128)} %copy-done, f32[512,8192]{1,0:T(8,128)} %fusion.33, f32[512,128]{0,1:T(8,128)S(1)} %fusion.34, f32[512,128]{0,1:T(8,128)S(1)} %fusion.46, f32[512,128]{0,1:T(8,128)S(1)} %fusion.44, f32[512,128]{0,1:T(8,128)S(1)} %fusion.42, bf16[8192,128]{1,0:T(8,128)(2,1)S(1)} %copy-done.3, ...), kind=kOutput, calls=%fused_computation.16 | convolution fusion | flops 4338483200 | bytes 59768832 | tf_op jit(solution)/shard_map/dot_general | solution.py:41
  564.7 6.7 abs_bitcast_fusion
  571.4 6.7 copy.33
  578.1 8.2 %reduce_max.19 = f32[512,64]{1,0:T(8,128)S(1)} reduce(f32[512,64,128]{2,1,0:T(8,128)} %bitcast.96, f32[]{:T(128)} %constant.43.clone.1), dimensions={2}, to_apply=%region_3.4 | reduce | flops 4161536 | bytes 16908292 | tf_op jit(solution)/shard_map/reduce_max | solution.py:14
  586.3 0.1 maximum_multiply_fusion
  586.4 0.8 copy.24
  587.1 3.5 all-to-all-start.4
  590.6 4.6 mul.86
  595.2 16.1 %fusion.3 = s16[512,8192]{1,0:T(8,128)(2,1)} fusion(f32[512,8192]{1,0:T(8,128)} %add_subtract_fusion, f32[64,8,64,128]{3,2,1,0:T(8,128)S(1)} %bitcast.97), kind=kLoop, calls=%fused_computation.7 | loop fusion | flops 16777216 | bytes 41943040 | tf_op jit(solution)/shard_map/convert_element_type | solution.py:17
  611.3 0.0 all-to-all-done.4
  611.3 5.9 all-to-all-start.3
  617.2 0.1 copy.25
  617.3 91.4 %all-to-all-done.3 = s16[4,128,8192]{2,1,0:T(8,128)(2,1)} async-done(((s16[4,128,8192]{2,1,0:T(8,128)(2,1)}), s16[4,128,8192]{2,1,0:T(8,128)(2,1)}, u32[]{:S(2)}, u32[]{:S(2)}) %all-to-all-start.3) | async-done | bytes 8388640 | tf_op jit(solution)/shard_map/all_to_all | solution.py:83
  708.7 12.3 %convert_bitcast_fusion = f32[4,16,8,8192]{3,2,1,0:T(8,128)} fusion(s16[4,128,8192]{2,1,0:T(8,128)(2,1)} %all-to-all-done.3), kind=kLoop, calls=%fused_computation.14 | loop fusion | flops 4194304 | bytes 25165824
  721.1 6.7 copy.29
  727.8 8.4 %mul.93 = f32[128,256,128]{2,1,0:T(8,128)} broadcast(f32[128,256]{1,0:T(8,128)S(1)} %copy.25), dimensions={0,1} | broadcast | bytes 16908288 | tf_op jit(solution)/shard_map/mul | solution.py:24
  736.2 18.1 %bitcast_multiply_fusion = f32[128,32768]{1,0:T(8,128)} fusion(f32[128,32768]{1,0:T(8,128)S(1)} %bitcast.93, f32[16,8,256,128]{3,2,1,0:T(8,128)} %bitcast.94), kind=kLoop, calls=%fused_computation.3 | loop fusion | flops 4194304 | bytes 50331648 | tf_op jit(solution)/shard_map/mul | solution.py:24
  (13 shorter events, 0.1 us)
Async XLA Ops:
  47.3 97.6 %all-to-all-start.2 = ((bf16[4,8192,128]{2,1,0:T(8,128)(2,1)}), bf16[4,8192,128]{2,1,0:T(8,128)(2,1)}, u32[]{:S(2)}, u32[]{:S(2)}) async-start(bf16[4,8192,128]{2,1,0:T(8,128)(2,1)} %bitcast.102), calls=%async_computation.2 | async-start | bytes 16777216 | tf_op jit(solution)/shard_map/all_to_all | solution.py:48
  144.9 4.3 copy-start.7
  144.9 12.2 %copy-start.8 = (s32[4]{0:T(128)S(1)}, s32[4]{0:T(128)}, u32[]{:S(2)}) copy-start(s32[4]{0:T(128)} %param.9) | copy-start | bytes 52
  144.9 192.1 %all-to-all-start = ((s16[16,32,8192]{2,0,1:T(8,128)(2,1)}), s16[16,32,8192]{2,0,1:T(8,128)(2,1)}, u32[]{:S(2)}, u32[]{:S(2)}) async-start(s16[16,32,8192]{2,0,1:T(8,128)(2,1)} %bitcast.101), calls=%async_computation | async-start | bytes 16777216 | tf_op jit(solution)/shard_map/all_to_all | solution.py:51
  148.7 375.1 %all-reduce.3.cloned.1.call-start = ((), (), s32[]{:S(2)}) async-start(), calls=%async_computation.5 | async-start | bytes 4194304 | tf_op jit(solution)/shard_map/psum | solution.py:70
  169.5 1.3 copy-start.1
  169.6 1.9 copy-start.4
  169.6 2.6 copy-start.5
  343.9 25.5 %copy-start.2 = (bf16[8192,128]{1,0:T(8,128)(2,1)S(1)}, bf16[8192,128]{1,0:T(8,128)(2,1)}, u32[]{:S(2)}) copy-start(bf16[8192,128]{1,0:T(8,128)(2,1)} %copy-done.1) | copy-start | bytes 6291460
  363.3 6.2 copy-start
  376.2 12.6 %copy-start.6 = (bf16[1,128,128]{2,1,0:T(8,128)(2,1)S(1)}, bf16[1,128,128]{2,1,0:T(8,128)(2,1)}, u32[]{:S(2)}) copy-start(bf16[1,128,128]{2,1,0:T(8,128)(2,1)} %param.7) | copy-start | bytes 98308
  535.1 10.3 %copy-start.3 = (bf16[8192,128]{1,0:T(8,128)(2,1)S(1)}, bf16[8192,128]{1,0:T(8,128)(2,1)}, u32[]{:S(2)}) copy-start(bf16[8192,128]{1,0:T(8,128)(2,1)} %copy-done.1) | copy-start | bytes 6291460
  587.1 24.1 %all-to-all-start.4 = ((f32[4,128,64]{1,2,0:T(8,128)}), f32[4,128,64]{1,2,0:T(8,128)S(1)}, u32[]{:S(2)}, u32[]{:S(2)}) async-start(f32[4,128,64]{1,2,0:T(8,128)} %copy.24), calls=%async_computation.4 | async-start | bytes 262144 | tf_op jit(solution)/shard_map/all_to_all | solution.py:84
  611.3 97.5 %all-to-all-start.3 = ((s16[4,128,8192]{2,1,0:T(8,128)(2,1)}), s16[4,128,8192]{2,1,0:T(8,128)(2,1)}, u32[]{:S(2)}, u32[]{:S(2)}) async-start(s16[4,128,8192]{2,1,0:T(8,128)(2,1)} %bitcast.99), calls=%async_computation.3 | async-start | bytes 16777216 | tf_op jit(solution)/shard_map/all_to_all | solution.py:83
Sparse Core Ops, SparseCore 0:
  388.9 134.8 all-reduce.2

commit v2 on v1

v2 whole, which is shorter than its diff:
```python
import functools

import jax
import jax.numpy as jnp
from jax import lax
from jax.experimental import pallas as pl
from jax.experimental.pallas import tpu as pltpu
from jax.sharding import PartitionSpec as P

PANELS = 4
GROUP = 128
CHUNK = 1024
TOP = 32767.0
FINE = 256.0
LN2 = 0.6931471805599453
VMEM_LIMIT = 56 * 1024 * 1024


def exponents(peaks):
    return jnp.ceil(jnp.log(jnp.maximum(peaks, 1e-30)) * (FINE / LN2))


def steps_of(code):
    return jnp.exp(code.astype(jnp.int32).astype(jnp.float32) * (LN2 / FINE)) * (1.0 / TOP)


def quantize(value, inverse):
    scaled = jnp.clip(jnp.round(value * inverse), -TOP, TOP)
    return scaled.astype(jnp.int32).astype(jnp.int16)


def as_float(code):
    return code.astype(jnp.int32).astype(jnp.float32)


def encode_kernel(x_ref, code_ref):
    rows, length = x_ref.shape
    lane = lax.broadcasted_iota(jnp.int32, (rows, GROUP), 1)
    peaks = jnp.zeros((rows, GROUP), jnp.float32)
    for g in range(length // GROUP):
        part = jnp.abs(x_ref[:, g * GROUP : (g + 1) * GROUP])
        peaks = jnp.where(lane == g, jnp.max(part, axis=1, keepdims=True), peaks)
    exponent = exponents(peaks)
    code_ref[:, length:] = exponent.astype(jnp.int32).astype(jnp.int16)
    inverse = jnp.exp(exponent * (-LN2 / FINE)) * TOP
    for g in range(length // GROUP):
        at = slice(g * GROUP, (g + 1) * GROUP)
        code_ref[:, at] = quantize(x_ref[:, at], inverse[:, g : g + 1])


def encode(eigvecs, parts):
    rows, columns = eigvecs.shape
    length = columns // parts
    return pl.pallas_call(
        encode_kernel,
        grid=(parts,),
        in_specs=[pl.BlockSpec((rows, length), lambda i: (0, i))],
        out_specs=pl.BlockSpec((None, rows, length + GROUP), lambda i: (i, 0, 0)),
        out_shape=jax.ShapeDtypeStruct((parts, rows, length + GROUP), jnp.int16),
        compiler_params=pltpu.CompilerParams(vmem_limit_bytes=VMEM_LIMIT),
        cost_estimate=pl.CostEstimate(
            flops=6 * rows * columns, bytes_accessed=6 * rows * columns, transcendentals=0
        ),
        name="encode",
    )(eigvecs)


def decoded_chunk(code_ref, steps, i):
    per = CHUNK // GROUP
    rolled = pltpu.roll(steps, lax.rem(GROUP - per * i, GROUP), 1)
    return [
        as_float(code_ref[:, pl.ds(pl.multiple_of(i * CHUNK + j * GROUP, GROUP), GROUP)])
        * rolled[:, j : j + 1]
        for j in range(per)
    ]


def project_kernel(code_ref, reflector_ref, out_ref, total):
    rows, length = out_ref.shape[0], reflector_ref.shape[0]
    steps = steps_of(code_ref[:, length:])
    total[...] = jnp.zeros_like(total)

    @pl.loop(0, length // CHUNK)
    def _(i):
        value = jnp.concatenate(decoded_chunk(code_ref, steps, i), axis=1)
        high = value.astype(jnp.bfloat16)
        low = (value - high.astype(jnp.float32)).astype(jnp.bfloat16)
        block = reflector_ref[pl.ds(pl.multiple_of(i * CHUNK, CHUNK), CHUNK), :]
        total[...] += jnp.dot(
            jnp.concatenate([high, low], axis=0), block, preferred_element_type=jnp.float32
        )

    out_ref[...] = total[:rows] + total[rows:]


def project(code, reflector, rows):
    count, width = code.shape
    length, reach = reflector.shape
    return pl.pallas_call(
        project_kernel,
        grid=(count // rows,),
        in_specs=[
            pl.BlockSpec((rows, width), lambda i: (i, 0)),
            pl.BlockSpec((length, reach), lambda i: (0, 0)),
        ],
        out_specs=pl.BlockSpec((rows, reach), lambda i: (i, 0)),
        out_shape=jax.ShapeDtypeStruct((count, reach), jnp.float32),
        scratch_shapes=[pltpu.VMEM((2 * rows, reach), jnp.float32)],
        compiler_params=pltpu.CompilerParams(vmem_limit_bytes=VMEM_LIMIT),
        cost_estimate=pl.CostEstimate(
            flops=4 * count * length * reach,
            bytes_accessed=2 * count * width + 2 * length * reach,
            transcendentals=0,
        ),
        name="project",
    )(code, reflector)


def update_kernel(code_ref, coeff_ref, reflector_ref, out_ref, field, peaks):
    rows, length = field.shape
    reach = reflector_ref.shape[1]
    per = CHUNK // GROUP
    steps = steps_of(code_ref[:, length:])
    lane = lax.broadcasted_iota(jnp.int32, (rows, GROUP), 1)
    coeffs = jnp.concatenate([coeff_ref[:, :reach], coeff_ref[:, reach:]], axis=0)
    peaks[...] = jnp.zeros_like(peaks)

    @pl.loop(0, length // CHUNK)
    def _(i):
        block = reflector_ref[pl.ds(pl.multiple_of(i * CHUNK, CHUNK), CHUNK), :]
        change = lax.dot_general(
            coeffs, block, (((1,), (1,)), ((), ())), preferred_element_type=jnp.float32
        )
        change = change[:rows] + change[rows:]
        top = peaks[...]
        for j, part in enumerate(decoded_chunk(code_ref, steps, i)):
            new = part - change[:, j * GROUP : (j + 1) * GROUP]
            field[:, pl.ds(pl.multiple_of(i * CHUNK + j * GROUP, GROUP), GROUP)] = new
            top = jnp.where(lane == i * per + j, jnp.max(jnp.abs(new), axis=1, keepdims=True), top)
        peaks[...] = top

    exponent = exponents(peaks[...])
    out_ref[:, length:] = exponent.astype(jnp.int32).astype(jnp.int16)
    inverse = jnp.exp(exponent * (-LN2 / FINE)) * TOP

    @pl.loop(0, length // CHUNK)
    def _(i):
        rolled = pltpu.roll(inverse, lax.rem(GROUP - per * i, GROUP), 1)
        for j in range(per):
            at = pl.ds(pl.multiple_of(i * CHUNK + j * GROUP, GROUP), GROUP)
            out_ref[:, at] = quantize(field[:, at], rolled[:, j : j + 1])


def update(code, coeffs, reflector, rows):
    count, width = code.shape
    length, reach = reflector.shape
    return pl.pallas_call(
        update_kernel,
        grid=(count // rows,),
        in_specs=[
            pl.BlockSpec((rows, width), lambda i: (i, 0)),
            pl.BlockSpec((rows, 2 * reach), lambda i: (i, 0)),
            pl.BlockSpec((length, reach), lambda i: (0, 0)),
        ],
        out_specs=pl.BlockSpec((rows, width), lambda i: (i, 0)),
        out_shape=jax.ShapeDtypeStruct((count, width), jnp.int16),
        scratch_shapes=[
            pltpu.VMEM((rows, length), jnp.float32),
            pltpu.VMEM((rows, GROUP), jnp.float32),
        ],
        compiler_params=pltpu.CompilerParams(vmem_limit_bytes=VMEM_LIMIT),
        cost_estimate=pl.CostEstimate(
            flops=4 * count * length * reach,
            bytes_accessed=4 * count * width + 2 * length * reach,
            transcendentals=0,
        ),
        name="update",
    )(code, coeffs, reflector)


def decode_kernel(code_ref, out_ref):
    length = out_ref.shape[1]
    steps = steps_of(code_ref[:, length:])

    @pl.loop(0, length // CHUNK)
    def _(i):
        for j, part in enumerate(decoded_chunk(code_ref, steps, i)):
            out_ref[:, pl.ds(pl.multiple_of(i * CHUNK + j * GROUP, GROUP), GROUP)] = part


def decode(code, parts):
    count, width = code.shape
    rows, length = count // parts, width - GROUP
    return pl.pallas_call(
        decode_kernel,
        grid=(parts,),
        in_specs=[pl.BlockSpec((rows, width), lambda i: (i, 0))],
        out_specs=pl.BlockSpec((rows, length), lambda i: (0, i)),
        out_shape=jax.ShapeDtypeStruct((rows, parts * length), jnp.float32),
        compiler_params=pltpu.CompilerParams(vmem_limit_bytes=VMEM_LIMIT),
        cost_estimate=pl.CostEstimate(
            flops=2 * count * length, bytes_accessed=6 * count * length, transcendentals=0
        ),
        name="decode",
    )(code)


def reflector_block(stored, offset, first_row):
    row_ids = first_row + lax.broadcasted_iota(jnp.int32, stored.shape, 0)
    col_ids = lax.broadcasted_iota(jnp.int32, stored.shape, 1)
    below = row_ids - col_ids - offset
    unit = jnp.where(below == 0, jnp.bfloat16(1.0), jnp.bfloat16(0.0))
    return jnp.where(below > 0, stored, unit)


def spread_panels(stored, n_col):
    length = stored.shape[0] // n_col
    me = lax.axis_index("col")
    pieces = []
    for k in range(n_col):
        to = lax.rem(me + k, n_col)
        piece = lax.dynamic_slice_in_dim(stored, to * length, length, axis=0)
        if k:
            piece = lax.ppermute(piece, "col", [(i, (i + k) % n_col) for i in range(n_col)])
        pieces.append(piece)
    return jnp.stack(pieces)


def local(eigvecs, panels, tfactors, owners, offsets):
    highest = lax.Precision.HIGHEST
    both = ("row", "col")
    n_row, n_col = lax.axis_size("row"), lax.axis_size("col")
    n_all = n_row * n_col
    me = lax.axis_index("col")
    stored = spread_panels(panels[0], n_col)
    triangles = lax.all_gather(tfactors[0], "col")
    code = encode(eigvecs, n_all)
    code = lax.all_to_all(code, both, split_axis=0, concat_axis=0, tiled=True)
    code = code.reshape(-1, code.shape[-1])
    count, rows = code.shape[0], code.shape[0] // n_col
    length = stored.shape[1]
    first_row = (lax.axis_index("row") * n_col + me) * length
    reflectors = [
        reflector_block(
            lax.dynamic_index_in_dim(
                stored, lax.rem(me - owners[panel] + n_col, n_col), 0, keepdims=False
            ),
            offsets[panel],
            first_row,
        )
        for panel in range(PANELS)
    ]
    reflector = jnp.concatenate(reflectors, axis=1)
    nb = reflector.shape[1] // PANELS
    gram = lax.psum(
        lax.dot_general(
            reflector, reflector, (((0,), (0,)), ((), ())), preferred_element_type=jnp.float32
        ),
        both,
    )
    identity = jnp.eye(PANELS * nb, dtype=jnp.float32)
    columns = [None] * PANELS
    for panel in reversed(range(PANELS)):
        at = slice(panel * nb, (panel + 1) * nb)
        inner = identity[:, at]
        for later in range(panel + 1, PANELS):
            block = gram[later * nb : (later + 1) * nb, at]
            inner = inner - jnp.dot(columns[later], block, precision=highest)
        triangle = lax.dynamic_index_in_dim(triangles, owners[panel], 0, keepdims=False)
        columns[panel] = jnp.dot(inner, triangle.astype(jnp.float32).T, precision=highest)
    mixing = jnp.concatenate(columns, axis=1)

    partial_sums = project(code, reflector, rows)
    partial_sums = lax.all_to_all(partial_sums, both, split_axis=0, concat_axis=0, tiled=True)
    projection = jnp.sum(partial_sums.reshape(n_all, count // n_all, -1), axis=0)
    coeffs = jnp.dot(projection, mixing, precision=highest)
    high = lax.reduce_precision(coeffs, 8, 7)
    pair = jnp.concatenate([high, coeffs - high], axis=1).astype(jnp.bfloat16)
    pair = lax.all_gather(pair, both, tiled=True)
    code = update(code, pair, reflector, rows)
    code = lax.all_to_all(code, "col", split_axis=0, concat_axis=0, tiled=True)
    return decode(code, n_col)


def solution(mesh):
    in_specs = (P(("row", "col"), None), P("col", "row", None), P("col", None, None), P(), P())
    out_specs = P("col", "row")
    return jax.shard_map(local, mesh=mesh, in_specs=in_specs, out_specs=out_specs, check_vma=False)
```

time: 770 us -> 628 us (0.82)
  waiting for transfers between devices: 433 us -> 158 us
  blocking collectives: 22.8 us -> 280 us
  other arithmetic: 130 us -> 13.8 us
  Pallas kernels: 0 us -> 102 us
  local copies, waits for them, and re-layouts: 69.9 us -> 10.7 us
  matrix products: 65.6 us -> 16.1 us
    all_to_all x4 -> x2, waiting for transfers between devices: 305 us -> 0.01 us  [the longest x1 0.01 us: local(): code = lax.all_to_all(code, both, split_axis=0, concat_axis=0, tiled=True)]
    all_gather x1, blocking collectives: 7.29 us -> 178 us  [local(): triangles = lax.all_gather(tfactors[0], 'col')]
    pallas_call x0 -> x4, Pallas kernels: none -> 102 us  [the longest x1 35.7 us: update(): pl.pallas_call(update_kernel, grid=(count // rows,), in_specs=[pl.BlockSp...]
    all_to_all x1, blocking collectives: 15.5 us -> 103 us  [local(): code = lax.all_to_all(code, 'col', split_axis=0, concat_axis=0, tiled=True)]
    all_gather x0 -> x1, waiting for transfers between devices: none -> 52.8 us  [local(): pair = lax.all_gather(pair, both, tiled=True)]
    dot_general x11 -> x8, matrix products: 63.5 us -> 15 us  [the longest x6 8.56 us: local(): inner = inner - jnp.dot(columns[later], block, precision=highest)]
    convert_element_type x2 -> x1, other arithmetic: 41.6 us -> 0.11 us  [local(): identity = jnp.eye(PANELS * nb, dtype=jnp.float32)]
    mul x3 -> x0, other arithmetic: 37.5 us -> none  [the longest x2 37.5 us: decode(): return (grouped * step[:, :, None]).reshape(rows, columns)]
  transfers between devices with their start and end apart: 5 -> 7, of which waited for: 4 -> 2; matrix products, arithmetic and copies ran while one was open for 10% -> 6% of each run, Pallas kernels for 0% -> 4%
where the time goes in v2:
time: 628 us; the launch traced here: 626 us
  blocking collectives  280 us (45%)
  waiting for transfers between devices  158 us (25%)
  Pallas kernels  102 us (16%)
  between operations  23.4 us (4%)
  starting transfers between devices  21.9 us (3%)
  matrix products  16.1 us (3%)
  other arithmetic  13.8 us (2%)
  local copies, waits for them, and re-layouts  10.7 us (2%)
    all_gather x1, blocking collectives, local(): triangles = lax.all_gather(tfactors[0], 'col')  178 us
    psum x1, waiting for transfers between devices, local(): lax.psum(lax.dot_general(reflector, reflector, (((0,), (0,)), ((), ())),...  105 us
    all_to_all x1, blocking collectives, local(): code = lax.all_to_all(code, 'col', split_axis=0, concat_axis=0, tiled=True)  103 us
    all_gather x1, waiting for transfers between devices, local(): pair = lax.all_gather(pair, both, tiled=True)  52.8 us
    pallas_call x1, Pallas kernels, update(): pl.pallas_call(update_kernel, grid=(count // rows,), in_specs=[pl.BlockSp...  35.7 us
    pallas_call x1, Pallas kernels, encode(): pl.pallas_call(encode_kernel, grid=(parts,), in_specs=[pl.BlockSpec((rows...  28.8 us
    pallas_call x1, Pallas kernels, project(): pl.pallas_call(project_kernel, grid=(count // rows,), in_specs=[pl.BlockS...  23.5 us
    pallas_call x1, Pallas kernels, decode(): pl.pallas_call(decode_kernel, grid=(parts,), in_specs=[pl.BlockSpec((rows...  13.8 us
  transfers between devices with their start and end apart: 7, of which 2 were waited for; matrix products, arithmetic and copies ran while one was open for 6% of the time, Pallas kernels for 4%

profile of v2, /device:TPU:0, one launch (start us, length us, event | category | flops | bytes accessed | tf_op | source)
XLA Modules:
  0.0 626.0 jit_solution(17592784413981721483)
XLA Ops:
  6.5 28.8 %encode.1 = s16[32,16,8320]{2,1,0:T(8,128)(2,1)} custom-call(f32[16,262144]{1,0:T(8,128)} %x_ref.1), custom_call_target="tpu_custom_call" | custom-call | flops 25165824 | bytes 25165824 | tf_op jit(solution)/shard_map/encode/pallas_call | solution.py:54
  35.4 7.4 %all-to-all-start = ((s16[32,16,8320]{2,1,0:T(8,128)(2,1)}), s16[32,16,8320]{2,1,0:T(8,128)(2,1)}, u32[]{:S(2)}, u32[]{:S(2)}) async-start(s16[32,16,8320]{2,1,0:T(8,128)(2,1)} %encode.1), calls=%async_computation | async-start | bytes 17039360 | tf_op jit(solution)/shard_map/all_to_all | solution.py:238
  42.8 0.0 all-reduce.2.cloned.1.call-start
  42.9 0.0 copy-start.2
  42.9 0.0 copy-start.1
  42.9 0.0 copy-start.3
  42.9 6.2 constant_dynamic-slice_fusion
  49.1 2.6 collective-permute-start.2
  51.7 0.6 collective-permute-start.1
  52.3 0.6 collective-permute-start
  52.8 0.0 copy-done.2
  52.8 0.6 fusion.55
  63.2 0.0 copy-done.1
  63.2 177.7 %all_gather.6 = bf16[4,128,128]{2,1,0:T(8,128)(2,1)S(1)} all-gather(bf16[1,128,128]{2,1,0:T(8,128)(2,1)S(1)} %copy-done.1), channel_id=1, replica_groups=mesh['row'=8,'col'=4] {'col'}, dimensions={0}, use_global_device_ids=true | all-gather | bytes 163840 | tf_op jit(solution)/shard_map/all_gather | solution.py:236
  240.9 0.0 copy-done.3
  240.9 0.6 fusion.54
  241.5 0.1 iota_compare_fusion
  241.6 0.1 fusion.28
  241.8 0.2 fusion.29
  242.0 0.0 collective-permute-done.2
  242.0 0.0 collective-permute-done.1
  242.0 0.0 collective-permute-done
  242.0 3.8 pad_maximum_fusion
  245.8 8.1 %fusion.18 = (bf16[8192,128]{1,0:T(8,128)(2,1)S(1)}, bf16[8192,128]{1,0:T(8,128)(2,1)S(1)}, bf16[8192,128]{1,0:T(8,128)(2,1)S(1)}, bf16[8192,128]{1,0:T(8,128)(2,1)S(1)}) fusion(bf16[4,8192,128]{2,1,0:T(8,128)(2,1)S(1)} %pad_maximum_fusion, s32[]{:T(128)S(6)} %select_n.68, s32[]{:T(128)} %bitcast.1, s32[8192]{0:T(1024)S(1)} %iota_add_fusion, ...), kind=kLoop, calls=%fused_computation.21 | loop fusion | flops 22020096 | bytes 16810016 | tf_op jit(solution)/shard_map/jit(_where)/select_n | solution.py:213
  254.0 1.0 pad_maximum_fusion.1.reflector_ref
  255.0 0.0 copy-start
  255.0 3.2 copy-done
  258.2 5.5 fusion.56
  263.7 0.0 all-reduce.2.cloned.1.call-update
  263.7 0.0 all-to-all-done
  263.7 23.5 %project.1 = f32[512,512]{1,0:T(8,128)} custom-call(s16[512,8320]{1,0:T(8,128)(2,1)} %bitcast.code_ref, bf16[8192,512]{1,0:T(8,128)(2,1)} %copy-done), custom_call_target="tpu_custom_call" | custom-call | flops 8589934592 | bytes 16908288 | tf_op jit(solution)/shard_map/project/pallas_call | solution.py:99
  287.2 10.5 %all-to-all-start.1 = ((f32[32,16,512]{2,1,0:T(8,128)}), f32[32,16,512]{2,1,0:T(8,128)S(1)}, u32[]{:S(2)}, u32[]{:S(2)}) async-start(f32[32,16,512]{2,1,0:T(8,128)} %bitcast.55), calls=%async_computation.1 | async-start | bytes 2097152 | tf_op jit(solution)/shard_map/all_to_all | solution.py:274
  297.7 0.2 all-gather.2.cloned.1.call-start
  297.9 105.1 %all-reduce.2.cloned.1.call-done = f32[512,512]{1,0:T(8,128)} async-done(((f32[512,512]{1,0:T(8,128)}), f32[512,512]{1,0:T(8,128)}) %all-reduce.2.cloned.1.call-update) | async-done | bytes 1048592 | tf_op jit(solution)/shard_map/psum | solution.py:255
  403.0 1.4 convolution_subtract_fusion.5
  404.5 0.3 fusion.42
  404.8 1.4 convolution_subtract_fusion.4
  406.2 1.4 convolution_subtract_fusion.3
  407.6 0.3 fusion.40
  407.9 1.4 convolution_subtract_fusion.2
  409.4 1.4 convolution_subtract_fusion.1
  410.8 1.4 convolution_subtract_fusion
  412.3 0.3 fusion.38
  412.6 0.0 all-to-all-done.1
  412.6 0.1 reduce_sum.9
  412.6 1.0 reduce-precision_convert_fusion
  413.6 0.6 pad_maximum_fusion.2
  414.2 0.0 all-gather.2.cloned.1.call-update
  414.3 52.8 %all-gather.2.cloned.1.call-done.coeff_ref = bf16[512,1024]{1,0:T(8,128)(2,1)} async-done(((bf16[16,1024]{1,0:T(8,128)(2,1)}), bf16[512,1024]{1,0:T(8,128)(2,1)}) %all-gather.2.cloned.1.call-update) | async-done | bytes 1048592 | tf_op jit(solution)/shard_map/all_gather | solution.py:279
  467.1 35.7 %update.1 = s16[512,8320]{1,0:T(8,128)(2,1)} custom-call(s16[512,8320]{1,0:T(8,128)(2,1)} %bitcast.code_ref, bf16[512,1024]{1,0:T(8,128)(2,1)} %all-gather.2.cloned.1.call-done.coeff_ref, bf16[8192,512]{1,0:T(8,128)(2,1)} %copy-done), custom_call_target="tpu_custom_call" | custom-call | flops 8589934592 | bytes 25427968 | tf_op jit(solution)/shard_map/update/pallas_call | solution.py:157
  502.8 102.5 %all_to_all.25 = s16[4,128,8320]{2,1,0:T(8,128)(2,1)} all-to-all(s16[4,128,8320]{2,1,0:T(8,128)(2,1)} %bitcast.54), channel_id=1, replica_groups=mesh['row'=8,'col'=4] {'col'}, dimensions={0} | all-to-all | bytes 17039360 | tf_op jit(solution)/shard_map/all_to_all | solution.py:281
  605.3 13.8 %decode.1 = f32[128,32768]{1,0:T(8,128)} custom-call(s16[512,8320]{1,0:T(8,128)(2,1)} %bitcast.53), custom_call_target="tpu_custom_call" | custom-call | flops 8388608 | bytes 25165824 | tf_op jit(solution)/shard_map/decode/pallas_call | solution.py:194
  (1 shorter events, 0.0 us)
Async XLA Ops:
  35.4 228.3 %all-to-all-start = ((s16[32,16,8320]{2,1,0:T(8,128)(2,1)}), s16[32,16,8320]{2,1,0:T(8,128)(2,1)}, u32[]{:S(2)}, u32[]{:S(2)}) async-start(s16[32,16,8320]{2,1,0:T(8,128)(2,1)} %encode.1), calls=%async_computation | async-start | bytes 17039360 | tf_op jit(solution)/shard_map/all_to_all | solution.py:238
  42.8 360.2 %all-reduce.2.cloned.1.call-start = ((), (), s32[]{:S(2)}) async-start(), calls=%async_computation.3 | async-start | bytes 2097152 | tf_op jit(solution)/shard_map/psum | solution.py:255
  42.9 10.0 %copy-start.2 = (s32[4]{0:T(128)S(1)}, s32[4]{0:T(128)}, u32[]{:S(2)}) copy-start(s32[4]{0:T(128)} %param.8) | copy-start | bytes 52
  42.9 20.3 %copy-start.1 = (bf16[1,128,128]{2,1,0:T(8,128)(2,1)S(1)}, bf16[1,128,128]{2,1,0:T(8,128)(2,1)}, u32[]{:S(2)}) copy-start(bf16[1,128,128]{2,1,0:T(8,128)(2,1)} %param.7) | copy-start | bytes 98308
  42.9 198.0 %copy-start.3 = (s32[4]{0:T(128)S(1)}, s32[4]{0:T(128)}, u32[]{:S(2)}) copy-start(s32[4]{0:T(128)} %param.9) | copy-start | bytes 52
  49.1 192.8 %collective-permute-start.2 = (bf16[8192,128]{1,0:T(8,128)(2,1)}, bf16[8192,128]{1,0:T(8,128)(2,1)}, u32[]{:S(2)}, u32[]{:S(2)}) collective-permute-start(bf16[8192,128]{1,0:T(8,128)(2,1)} %get-tuple-element.11), channel_id=1, source_target_pairs={{0,3},{1,0},{2,1},{3,2},{4,7},{5,4},{6,5},{7,6},{8,11},{9,8},{10,9... | collective-permute-start | bytes 6291464 | tf_op jit(solution)/shard_map/ppermute | solution.py:224
  51.7 190.3 %collective-permute-start.1 = (bf16[8192,128]{1,0:T(8,128)(2,1)}, bf16[8192,128]{1,0:T(8,128)(2,1)}, u32[]{:S(2)}, u32[]{:S(2)}) collective-permute-start(bf16[8192,128]{1,0:T(8,128)(2,1)} %get-tuple-element.12), channel_id=1, source_target_pairs={{0,2},{1,3},{2,0},{3,1},{4,6},{5,7},{6,4},{7,5},{8,10},{9,11},{10,... | collective-permute-start | bytes 6291464 | tf_op jit(solution)/shard_map/ppermute | solution.py:224
  52.3 189.7 %collective-permute-start = (bf16[8192,128]{1,0:T(8,128)(2,1)}, bf16[8192,128]{1,0:T(8,128)(2,1)}, u32[]{:S(2)}, u32[]{:S(2)}) collective-permute-start(bf16[8192,128]{1,0:T(8,128)(2,1)} %get-tuple-element.10), channel_id=1, source_target_pairs={{0,1},{1,2},{2,3},{3,0},{4,5},{5,6},{6,7},{7,4},{8,9},{9,10},{10,1... | collective-permute-start | bytes 6291464 | tf_op jit(solution)/shard_map/ppermute | solution.py:224
  255.0 3.2 copy-start
  287.2 125.4 %all-to-all-start.1 = ((f32[32,16,512]{2,1,0:T(8,128)}), f32[32,16,512]{2,1,0:T(8,128)S(1)}, u32[]{:S(2)}, u32[]{:S(2)}) async-start(f32[32,16,512]{2,1,0:T(8,128)} %bitcast.55), calls=%async_computation.1 | async-start | bytes 2097152 | tf_op jit(solution)/shard_map/all_to_all | solution.py:274
  297.7 169.5 %all-gather.2.cloned.1.call-start = ((), (), s32[]{:S(2)}) async-start(), calls=%async_computation.4 | async-start | bytes 1081344 | tf_op jit(solution)/shard_map/all_gather | solution.py:279
Sparse Core Ops, SparseCore 0:
  263.8 139.1 all-reduce.1
  414.4 52.6 all-gather.1

commit v3 on v2

--- a/solution.py
+++ b/solution.py
@@ -35,26 +35,24 @@
 
 def encode_kernel(x_ref, code_ref):
     rows, length = x_ref.shape
-    lane = lax.broadcasted_iota(jnp.int32, (rows, GROUP), 1)
     peaks = jnp.zeros((rows, GROUP), jnp.float32)
     for g in range(length // GROUP):
-        part = jnp.abs(x_ref[:, g * GROUP : (g + 1) * GROUP])
-        peaks = jnp.where(lane == g, jnp.max(part, axis=1, keepdims=True), peaks)
+        peaks = jnp.maximum(peaks, jnp.abs(x_ref[:, g * GROUP : (g + 1) * GROUP]))
     exponent = exponents(peaks)
     code_ref[:, length:] = exponent.astype(jnp.int32).astype(jnp.int16)
     inverse = jnp.exp(exponent * (-LN2 / FINE)) * TOP
     for g in range(length // GROUP):
         at = slice(g * GROUP, (g + 1) * GROUP)
-        code_ref[:, at] = quantize(x_ref[:, at], inverse[:, g : g + 1])
-
-
-def encode(eigvecs, parts):
+        code_ref[:, at] = quantize(x_ref[:, at], inverse)
+
+
+def encode(eigvecs, parts, half, halves):
     rows, columns = eigvecs.shape
-    length = columns // parts
+    rows, length = rows // halves, columns // parts
     return pl.pallas_call(
         encode_kernel,
         grid=(parts,),
-        in_specs=[pl.BlockSpec((rows, length), lambda i: (0, i))],
+        in_specs=[pl.BlockSpec((rows, length), lambda i: (half, i))],
         out_specs=pl.BlockSpec((None, rows, length + GROUP), lambda i: (i, 0, 0)),
         out_shape=jax.ShapeDtypeStruct((parts, rows, length + GROUP), jnp.int16),
         compiler_params=pltpu.CompilerParams(vmem_limit_bytes=VMEM_LIMIT),
@@ -65,13 +63,14 @@
     )(eigvecs)
 
 
+def lanes(start):
+    return pl.ds(pl.multiple_of(start, GROUP), GROUP)
+
+
 def decoded_chunk(code_ref, steps, i):
-    per = CHUNK // GROUP
-    rolled = pltpu.roll(steps, lax.rem(GROUP - per * i, GROUP), 1)
     return [
-        as_float(code_ref[:, pl.ds(pl.multiple_of(i * CHUNK + j * GROUP, GROUP), GROUP)])
-        * rolled[:, j : j + 1]
-        for j in range(per)
+        as_float(code_ref[:, lanes(i * CHUNK + j * GROUP)]) * steps
+        for j in range(CHUNK // GROUP)
     ]
 
 
@@ -119,9 +118,7 @@
 def update_kernel(code_ref, coeff_ref, reflector_ref, out_ref, field, peaks):
     rows, length = field.shape
     reach = reflector_ref.shape[1]
-    per = CHUNK // GROUP
     steps = steps_of(code_ref[:, length:])
-    lane = lax.broadcasted_iota(jnp.int32, (rows, GROUP), 1)
     coeffs = jnp.concatenate([coeff_ref[:, :reach], coeff_ref[:, reach:]], axis=0)
     peaks[...] = jnp.zeros_like(peaks)
 
@@ -135,8 +132,8 @@
         top = peaks[...]
         for j, part in enumerate(decoded_chunk(code_ref, steps, i)):
             new = part - change[:, j * GROUP : (j + 1) * GROUP]
-            field[:, pl.ds(pl.multiple_of(i * CHUNK + j * GROUP, GROUP), GROUP)] = new
-            top = jnp.where(lane == i * per + j, jnp.max(jnp.abs(new), axis=1, keepdims=True), top)
+            field[:, lanes(i * CHUNK + j * GROUP)] = new
+            top = jnp.maximum(top, jnp.abs(new))
         peaks[...] = top
 
     exponent = exponents(peaks[...])
@@ -145,10 +142,9 @@
 
     @pl.loop(0, length // CHUNK)
     def _(i):
-        rolled = pltpu.roll(inverse, lax.rem(GROUP - per * i, GROUP), 1)
-        for j in range(per):
-            at = pl.ds(pl.multiple_of(i * CHUNK + j * GROUP, GROUP), GROUP)
-            out_ref[:, at] = quantize(field[:, at], rolled[:, j : j + 1])
+        for j in range(CHUNK // GROUP):
+            at = lanes(i * CHUNK + j * GROUP)
+            out_ref[:, at] = quantize(field[:, at], inverse)
 
 
 def update(code, coeffs, reflector, rows):
@@ -178,31 +174,39 @@
     )(code, coeffs, reflector)
 
 
-def decode_kernel(code_ref, out_ref):
-    length = out_ref.shape[1]
-    steps = steps_of(code_ref[:, length:])
-
-    @pl.loop(0, length // CHUNK)
-    def _(i):
-        for j, part in enumerate(decoded_chunk(code_ref, steps, i)):
-            out_ref[:, pl.ds(pl.multiple_of(i * CHUNK + j * GROUP, GROUP), GROUP)] = part
-
-
-def decode(code, parts):
-    count, width = code.shape
+def decode_kernel(run, *refs):
+    out_ref, code_refs = refs[-1], refs[:-1]
+    length, halves = out_ref.shape[1], len(code_refs)
+    for half, code_ref in enumerate(code_refs):
+        steps = steps_of(code_ref[:, length:])
+
+        @pl.loop(0, length // CHUNK)
+        def _(i):
+            for j, part in enumerate(decoded_chunk(code_ref, steps, i)):
+                at = lanes(i * CHUNK + j * GROUP)
+                for k in range(part.shape[0] // run):
+                    to = (k * halves + half) * run
+                    out_ref[to : to + run, at] = part[k * run : (k + 1) * run]
+
+
+def decode(codes, parts, run):
+    count, width = codes[0].shape
     rows, length = count // parts, width - GROUP
+    total = rows * len(codes)
     return pl.pallas_call(
-        decode_kernel,
+        functools.partial(decode_kernel, rows if len(codes) == 1 else run),
         grid=(parts,),
-        in_specs=[pl.BlockSpec((rows, width), lambda i: (i, 0))],
-        out_specs=pl.BlockSpec((rows, length), lambda i: (0, i)),
-        out_shape=jax.ShapeDtypeStruct((rows, parts * length), jnp.float32),
+        in_specs=[pl.BlockSpec((rows, width), lambda i: (i, 0)) for _ in codes],
+        out_specs=pl.BlockSpec((total, length), lambda i: (0, i)),
+        out_shape=jax.ShapeDtypeStruct((total, parts * length), jnp.float32),
         compiler_params=pltpu.CompilerParams(vmem_limit_bytes=VMEM_LIMIT),
         cost_estimate=pl.CostEstimate(
-            flops=2 * count * length, bytes_accessed=6 * count * length, transcendentals=0
+            flops=2 * total * parts * length,
+            bytes_accessed=6 * total * parts * length,
+            transcendentals=0,
         ),
         name="decode",
-    )(code)
+    )(*codes)
 
 
 def reflector_block(stored, offset, first_row):
@@ -234,10 +238,15 @@
     me = lax.axis_index("col")
     stored = spread_panels(panels[0], n_col)
     triangles = lax.all_gather(tfactors[0], "col")
-    code = encode(eigvecs, n_all)
-    code = lax.all_to_all(code, both, split_axis=0, concat_axis=0, tiled=True)
-    code = code.reshape(-1, code.shape[-1])
-    count, rows = code.shape[0], code.shape[0] // n_col
+    mine = eigvecs.shape[0]
+    halves = 2 if mine % 16 == 0 else 1
+    run = mine // halves
+    codes = []
+    for half in range(halves):
+        code = encode(eigvecs, n_all, half, halves)
+        code = lax.all_to_all(code, both, split_axis=0, concat_axis=0, tiled=True)
+        codes.append(code.reshape(n_all * run, code.shape[-1]))
+    rows = n_row * run
     length = stored.shape[1]
     first_row = (lax.axis_index("row") * n_col + me) * length
     reflectors = [
@@ -252,34 +261,38 @@
     ]
     reflector = jnp.concatenate(reflectors, axis=1)
     nb = reflector.shape[1] // PANELS
-    gram = lax.psum(
-        lax.dot_general(
-            reflector, reflector, (((0,), (0,)), ((), ())), preferred_element_type=jnp.float32
-        ),
-        both,
+    sums = lax.dot_general(
+        reflector, reflector, (((0,), (0,)), ((), ())), preferred_element_type=jnp.float32
     )
+    pairs = [(q, p) for p in range(PANELS) for q in range(p + 1, PANELS)]
+    sums = [sums[q * nb : (q + 1) * nb, p * nb : (p + 1) * nb] for q, p in pairs]
+    sums = lax.psum(jnp.concatenate(sums, axis=0), both)
+    gram = {pair: sums[i * nb : (i + 1) * nb] for i, pair in enumerate(pairs)}
     identity = jnp.eye(PANELS * nb, dtype=jnp.float32)
     columns = [None] * PANELS
     for panel in reversed(range(PANELS)):
         at = slice(panel * nb, (panel + 1) * nb)
         inner = identity[:, at]
         for later in range(panel + 1, PANELS):
-            block = gram[later * nb : (later + 1) * nb, at]
-            inner = inner - jnp.dot(columns[later], block, precision=highest)
+            inner = inner - jnp.dot(columns[later], gram[later, panel], precision=highest)
         triangle = lax.dynamic_index_in_dim(triangles, owners[panel], 0, keepdims=False)
         columns[panel] = jnp.dot(inner, triangle.astype(jnp.float32).T, precision=highest)
     mixing = jnp.concatenate(columns, axis=1)
 
-    partial_sums = project(code, reflector, rows)
-    partial_sums = lax.all_to_all(partial_sums, both, split_axis=0, concat_axis=0, tiled=True)
-    projection = jnp.sum(partial_sums.reshape(n_all, count // n_all, -1), axis=0)
-    coeffs = jnp.dot(projection, mixing, precision=highest)
-    high = lax.reduce_precision(coeffs, 8, 7)
-    pair = jnp.concatenate([high, coeffs - high], axis=1).astype(jnp.bfloat16)
-    pair = lax.all_gather(pair, both, tiled=True)
-    code = update(code, pair, reflector, rows)
-    code = lax.all_to_all(code, "col", split_axis=0, concat_axis=0, tiled=True)
-    return decode(code, n_col)
+    for half in range(halves):
+        part = project(codes[half], reflector, rows)
+        if half < halves - 1:
+            projection = lax.psum_scatter(part, both, scatter_dimension=0, tiled=True)
+        else:
+            part = lax.all_to_all(part, both, split_axis=0, concat_axis=0, tiled=True)
+            projection = jnp.sum(part.reshape(n_all, run, -1), axis=0)
+        coeffs = jnp.dot(projection, mixing, precision=highest)
+        high = lax.reduce_precision(coeffs, 8, 7)
+        pair = jnp.concatenate([high, coeffs - high], axis=1).astype(jnp.bfloat16)
+        pair = lax.all_gather(pair, both, tiled=True)
+        code = update(codes[half], pair, reflector, rows)
+        codes[half] = lax.all_to_all(code, "col", split_axis=0, concat_axis=0, tiled=True)
+    return decode(codes, n_col, run)
 
 
 def solution(mesh):

time: 628 us -> 856 us (1.36)
  waiting for transfers between devices: 158 us -> 408 us
  blocking collectives: 280 us -> 221 us
  Pallas kernels: 102 us -> 125 us
    all_gather x1, blocking collectives: 178 us -> 26.4 us  [local(): triangles = lax.all_gather(tfactors[0], 'col')]
    all_gather x0 -> x2, blocking collectives: none -> 144 us  [local(): pair = lax.all_gather(pair, both, tiled=True)]
    reduce_scatter x0 -> x1, waiting for transfers between devices: none -> 133 us  [local(): projection = lax.psum_scatter(part, both, scatter_dimension=0, tiled=True)]
    ppermute x3, waiting for transfers between devices: 0.01 us -> 131 us  [spread_panels(): lax.ppermute(piece, 'col', [(i, (i + k) % n_col) for i in range(n_col)])]
    all_gather x1 -> x0, waiting for transfers between devices: 52.8 us -> none  [local(): pair = lax.all_gather(pair, both, tiled=True)]
    all_to_all x1, blocking collectives: 103 us -> 50.2 us  [local(): lax.all_to_all(code, 'col', split_axis=0, concat_axis=0, tiled=True)]
    psum x1, waiting for transfers between devices: 105 us -> 144 us  [local(): sums = lax.psum(jnp.concatenate(sums, axis=0), both)]
    pallas_call x1 -> x2, Pallas kernels: 28.8 us -> 39.6 us  [encode(): pl.pallas_call(encode_kernel, grid=(parts,), in_specs=[pl.BlockSpec((rows...]
  transfers between devices with their start and end apart: 7 -> 9, of which waited for: 2 -> 5; matrix products, arithmetic and copies ran while one was open for 6% -> 5% of each run, Pallas kernels for 4% -> 9%
where the time goes in v3:
time: 856 us; the launch traced here: 854 us
  waiting for transfers between devices  408 us (48%)
  blocking collectives  221 us (26%)
  Pallas kernels  125 us (15%)
  starting transfers between devices  29.4 us (3%)
  between operations  23.6 us (3%)
  matrix products  21.8 us (3%)
  other arithmetic  16.9 us (2%)
    all_gather x2, blocking collectives, local(): pair = lax.all_gather(pair, both, tiled=True)  144 us
    psum x1, waiting for transfers between devices, local(): sums = lax.psum(jnp.concatenate(sums, axis=0), both)  144 us
    reduce_scatter x1, waiting for transfers between devices, local(): projection = lax.psum_scatter(part, both, scatter_dimension=0, tiled=True)  133 us
    ppermute x3, waiting for transfers between devices, spread_panels(): lax.ppermute(piece, 'col', [(i, (i + k) % n_col) for i in range(n_col)])  131 us
    all_to_all x1, blocking collectives, local(): lax.all_to_all(code, 'col', split_axis=0, concat_axis=0, tiled=True)  50.2 us
    pallas_call x2, Pallas kernels, update(): pl.pallas_call(update_kernel, grid=(count // rows,), in_specs=[pl.BlockSp...  46.1 us
    pallas_call x2, Pallas kernels, encode(): pl.pallas_call(encode_kernel, grid=(parts,), in_specs=[pl.BlockSpec((rows...  39.6 us
    pallas_call x2, Pallas kernels, project(): pl.pallas_call(project_kernel, grid=(count // rows,), in_specs=[pl.BlockS...  29.3 us
  transfers between devices with their start and end apart: 9, of which 5 were waited for; matrix products, arithmetic and copies ran while one was open for 5% of the time, Pallas kernels for 9%

profile of v3, /device:TPU:0, one launch (start us, length us, event | category | flops | bytes accessed | tf_op | source)
XLA Modules:
  0.0 853.8 jit_solution(11206770666700247554)
XLA Ops:
  6.5 19.8 %encode.3 = s16[32,8,8320]{2,1,0:T(8,128)(2,1)} custom-call(f32[16,262144]{1,0:T(8,128)} %x_ref.3), custom_call_target="tpu_custom_call" | custom-call | flops 12582912 | bytes 12582912 | tf_op jit(solution)/shard_map/encode/pallas_call | solution.py:52
  26.4 7.4 all-to-all-start.2
  33.8 0.0 copy-start.1
  33.8 0.0 copy-start.2
  33.8 6.3 constant_dynamic-slice_fusion
  40.2 1.7 collective-permute-start
  41.9 1.5 collective-permute-start.1
  43.3 1.5 collective-permute-start.2
  44.8 0.0 copy-done.1
  44.8 0.6 fusion.51
  48.0 0.0 copy-done.2
  48.0 0.7 fusion.50
  48.6 87.3 %collective-permute-done = bf16[8192,128]{1,0:T(8,128)(2,1)} collective-permute-done((bf16[8192,128]{1,0:T(8,128)(2,1)}, bf16[8192,128]{1,0:T(8,128)(2,1)}, u32[]{:S(2)}, u32[]{:S(2)}) %collective-permute-start) | collective-permute-done | bytes 2097184 | tf_op jit(solution)/shard_map/ppermute | solution.py:228
  135.9 36.3 %collective-permute-done.1 = bf16[8192,128]{1,0:T(8,128)(2,1)} collective-permute-done((bf16[8192,128]{1,0:T(8,128)(2,1)}, bf16[8192,128]{1,0:T(8,128)(2,1)}, u32[]{:S(2)}, u32[]{:S(2)}) %collective-permute-start.1) | collective-permute-done | bytes 2097184 | tf_op jit(solution)/shard_map/ppermute | solution.py:228
  172.2 7.4 collective-permute-done.2
  179.6 3.8 pad_maximum_fusion
  183.5 8.2 fusion.18
  191.7 3.8 pad_maximum_fusion.1.reflector_ref
  195.5 0.0 all-to-all-done.2
  195.5 14.7 %project.3 = f32[256,512]{1,0:T(8,128)} custom-call(s16[256,8320]{1,0:T(8,128)(2,1)} %bitcast.25.code_ref, bf16[8192,512]{1,0:T(8,128)(2,1)} %pad_maximum_fusion.1.reflector_ref), custom_call_target="tpu_custom_call" | custom-call | flops 4294967296 | bytes 12648448 | tf_op jit(solution)/shard_map/project/pallas_call | solution.py:98
  210.1 6.5 all-to-all-start.3
  216.6 19.8 %encode.2 = s16[32,8,8320]{2,1,0:T(8,128)(2,1)} custom-call(f32[16,262144]{1,0:T(8,128)} %x_ref.3), custom_call_target="tpu_custom_call" | custom-call | flops 12582912 | bytes 12582912 | tf_op jit(solution)/shard_map/encode/pallas_call | solution.py:52
  236.4 0.0 copy-start
  236.4 0.0 all-to-all-done.3
  236.4 5.9 all-to-all-start
  242.4 0.0 all-reduce.2.cloned.1.call-start
  249.8 0.0 copy-done
  249.8 26.4 %all_gather.9 = bf16[4,128,128]{2,1,0:T(8,128)(2,1)S(1)} all-gather(bf16[1,128,128]{2,1,0:T(8,128)(2,1)S(1)} %copy-done), channel_id=1, replica_groups=mesh['row'=8,'col'=4] {'col'}, dimensions={0}, use_global_device_ids=true | all-gather | bytes 163840 | tf_op jit(solution)/shard_map/all_gather | solution.py:240
  276.3 0.1 iota_compare_fusion
  276.4 0.1 fusion.22
  276.5 9.5 %fusion.52 = f32[512,512]{1,0:T(8,128)S(1)} fusion(bf16[8192,512]{1,0:T(8,128)(2,1)} %pad_maximum_fusion.1.reflector_ref), kind=kOutput, calls=%fused_computation.75 | convolution fusion | flops 4294967296 | bytes 9437184 | tf_op jit(solution)/shard_map/dot_general | solution.py:264
  286.1 0.8 pad_maximum_fusion.5
  286.9 0.0 all-reduce.2.cloned.1.call-update
  286.9 0.2 fusion.23
  287.1 143.7 %all-reduce.2.cloned.1.call-done = f32[768,128]{1,0:T(8,128)} async-done(((f32[768,128]{1,0:T(8,128)}), f32[768,128]{1,0:T(8,128)}) %all-reduce.2.cloned.1.call-update) | async-done | bytes 393232 | tf_op jit(solution)/shard_map/psum | solution.py:269
  430.8 1.4 convolution_subtract_fusion.5
  432.2 0.3 fusion.35
  432.5 1.4 convolution_subtract_fusion.4
  434.0 1.4 convolution_subtract_fusion.3
  435.4 0.3 fusion.33
  435.7 1.4 convolution_subtract_fusion.2
  437.1 1.4 convolution_subtract_fusion.1
  438.6 1.4 convolution_subtract_fusion
  440.0 0.3 fusion.31
  440.4 1.0 reduce-precision_convert_fusion
  441.3 73.0 %all_gather.11.coeff_ref = bf16[256,1024]{1,0:T(8,128)(2,1)} all-gather(bf16[8,1024]{1,0:T(8,128)(2,1)S(1)} %pad_maximum_fusion.7), channel_id=1, replica_groups=mesh['row'=8,'col'=4] {'row','col'}, dimensions={0}, use_global_device_ids=true | all-gather | bytes 540672 | tf_op jit(solution)/shard_map/all_gather | solution.py:292
  514.4 23.1 %update.3 = s16[256,8320]{1,0:T(8,128)(2,1)} custom-call(s16[256,8320]{1,0:T(8,128)(2,1)} %bitcast.25.code_ref, bf16[256,1024]{1,0:T(8,128)(2,1)} %all_gather.11.coeff_ref, bf16[8192,512]{1,0:T(8,128)(2,1)} %pad_maximum_fusion.1.reflector_ref), custom_call_target="tpu_custom_call" | custom-call | flops 4294967296 | bytes 16908288 | tf_op jit(solution)/shard_map/update/pallas_call | solution.py:153
  537.4 0.0 all-to-all-done
  537.4 4.9 all-to-all-start.4
  542.3 0.0 reduce-scatter.2.cloned.1.call-start
  542.4 14.7 %project.2 = f32[256,512]{1,0:T(8,128)} custom-call(s16[256,8320]{1,0:T(8,128)(2,1)} %bitcast.code_ref, bf16[8192,512]{1,0:T(8,128)(2,1)} %pad_maximum_fusion.1.reflector_ref), custom_call_target="tpu_custom_call" | custom-call | flops 4294967296 | bytes 12648448 | tf_op jit(solution)/shard_map/project/pallas_call | solution.py:98
  557.0 0.0 reduce-scatter.2.cloned.1.call-update
  557.0 133.4 %reduce-scatter.2.cloned.1.call-done = f32[8,512]{1,0:T(8,128)} async-done(((f32[256,512]{1,0:T(8,128)}), f32[8,512]{1,0:T(8,128)}) %reduce-scatter.2.cloned.1.call-update) | async-done | bytes 16400 | tf_op jit(solution)/shard_map/reduce_scatter | solution.py:285
  690.4 1.7 reduce-precision_convert_fusion.1
  692.1 71.2 %all_gather.10.coeff_ref = bf16[256,1024]{1,0:T(8,128)(2,1)} all-gather(bf16[8,1024]{1,0:T(8,128)(2,1)S(1)} %pad_maximum_fusion.6), channel_id=1, replica_groups=mesh['row'=8,'col'=4] {'row','col'}, dimensions={0}, use_global_device_ids=true | all-gather | bytes 540672 | tf_op jit(solution)/shard_map/all_gather | solution.py:292
  763.3 23.1 %update.2 = s16[256,8320]{1,0:T(8,128)(2,1)} custom-call(s16[256,8320]{1,0:T(8,128)(2,1)} %bitcast.code_ref, bf16[256,1024]{1,0:T(8,128)(2,1)} %all_gather.10.coeff_ref, bf16[8192,512]{1,0:T(8,128)(2,1)} %pad_maximum_fusion.1.reflector_ref), custom_call_target="tpu_custom_call" | custom-call | flops 4294967296 | bytes 16908288 | tf_op jit(solution)/shard_map/update/pallas_call | solution.py:153
  786.4 0.0 all-to-all-done.4
  786.4 50.2 %all_to_all.41 = s16[4,64,8320]{2,1,0:T(8,128)(2,1)} all-to-all(s16[4,64,8320]{2,1,0:T(8,128)(2,1)} %bitcast.58), channel_id=1, replica_groups=mesh['row'=8,'col'=4] {'col'}, dimensions={0} | all-to-all | bytes 8519680 | tf_op jit(solution)/shard_map/all_to_all | solution.py:294
  836.6 10.4 %decode.1 = f32[128,32768]{1,0:T(8,128)} custom-call(s16[256,8320]{1,0:T(8,128)(2,1)} %bitcast.59, s16[256,8320]{1,0:T(8,128)(2,1)} %bitcast.28.refs_1_), custom_call_target="tpu_custom_call" | custom-call | flops 8388608 | bytes 25165824 | tf_op jit(solution)/shard_map/decode/pallas_call | solution.py:196
  (7 shorter events, 0.1 us)
Async XLA Ops:
  26.4 169.1 %all-to-all-start.2 = ((s16[32,8,8320]{2,1,0:T(8,128)(2,1)}), s16[32,8,8320]{2,1,0:T(8,128)(2,1)}, u32[]{:S(2)}, u32[]{:S(2)}) async-start(s16[32,8,8320]{2,1,0:T(8,128)(2,1)} %encode.3), calls=%async_computation.3 | async-start | bytes 8519680 | tf_op jit(solution)/shard_map/all_to_all | solution.py:247
  33.8 11.0 %copy-start.1 = (s32[4]{0:T(128)S(1)}, s32[4]{0:T(128)}, u32[]{:S(2)}) copy-start(s32[4]{0:T(128)} %param.8) | copy-start | bytes 52
  33.8 14.1 %copy-start.2 = (s32[4]{0:T(128)S(1)}, s32[4]{0:T(128)}, u32[]{:S(2)}) copy-start(s32[4]{0:T(128)} %param.9) | copy-start | bytes 52
  40.2 95.7 %collective-permute-start = (bf16[8192,128]{1,0:T(8,128)(2,1)}, bf16[8192,128]{1,0:T(8,128)(2,1)}, u32[]{:S(2)}, u32[]{:S(2)}) collective-permute-start(bf16[8192,128]{1,0:T(8,128)(2,1)} %get-tuple-element.10), channel_id=1, source_target_pairs={{0,1},{1,2},{2,3},{3,0},{4,5},{5,6},{6,7},{7,4},{8,9},{9,10},{10,1... | collective-permute-start | bytes 6291464 | tf_op jit(solution)/shard_map/ppermute | solution.py:228
  41.9 130.3 %collective-permute-start.1 = (bf16[8192,128]{1,0:T(8,128)(2,1)}, bf16[8192,128]{1,0:T(8,128)(2,1)}, u32[]{:S(2)}, u32[]{:S(2)}) collective-permute-start(bf16[8192,128]{1,0:T(8,128)(2,1)} %get-tuple-element.12), channel_id=1, source_target_pairs={{0,2},{1,3},{2,0},{3,1},{4,6},{5,7},{6,4},{7,5},{8,10},{9,11},{10,... | collective-permute-start | bytes 6291464 | tf_op jit(solution)/shard_map/ppermute | solution.py:228
  43.3 136.3 %collective-permute-start.2 = (bf16[8192,128]{1,0:T(8,128)(2,1)}, bf16[8192,128]{1,0:T(8,128)(2,1)}, u32[]{:S(2)}, u32[]{:S(2)}) collective-permute-start(bf16[8192,128]{1,0:T(8,128)(2,1)} %get-tuple-element.11), channel_id=1, source_target_pairs={{0,3},{1,0},{2,1},{3,2},{4,7},{5,4},{6,5},{7,6},{8,11},{9,8},{10,9... | collective-permute-start | bytes 6291464 | tf_op jit(solution)/shard_map/ppermute | solution.py:228
  210.1 26.3 %all-to-all-start.3 = ((f32[32,8,512]{2,1,0:T(8,128)}), f32[32,8,512]{2,1,0:T(8,128)S(1)}, u32[]{:S(2)}, u32[]{:S(2)}) async-start(f32[32,8,512]{2,1,0:T(8,128)} %bitcast.60), calls=%async_computation.4 | async-start | bytes 1048576 | tf_op jit(solution)/shard_map/all_to_all | solution.py:287
  236.4 13.4 %copy-start = (bf16[1,128,128]{2,1,0:T(8,128)(2,1)S(1)}, bf16[1,128,128]{2,1,0:T(8,128)(2,1)}, u32[]{:S(2)}) copy-start(bf16[1,128,128]{2,1,0:T(8,128)(2,1)} %param.7) | copy-start | bytes 98308
  236.4 301.0 %all-to-all-start = ((s16[32,8,8320]{2,1,0:T(8,128)(2,1)}), s16[32,8,8320]{2,1,0:T(8,128)(2,1)}, u32[]{:S(2)}, u32[]{:S(2)}) async-start(s16[32,8,8320]{2,1,0:T(8,128)(2,1)} %encode.2), calls=%async_computation | async-start | bytes 8519680 | tf_op jit(solution)/shard_map/all_to_all | solution.py:247
  242.4 188.4 %all-reduce.2.cloned.1.call-start = ((), (), s32[]{:S(2)}) async-start(), calls=%async_computation.7 | async-start | bytes 786432 | tf_op jit(solution)/shard_map/psum | solution.py:269
  537.4 249.0 %all-to-all-start.4 = ((s16[4,64,8320]{2,1,0:T(8,128)(2,1)}), s16[4,64,8320]{2,1,0:T(8,128)(2,1)}, u32[]{:S(2)}, u32[]{:S(2)}) async-start(s16[4,64,8320]{2,1,0:T(8,128)(2,1)} %bitcast.57), calls=%async_computation.5 | async-start | bytes 8519680 | tf_op jit(solution)/shard_map/all_to_all | solution.py:294
  542.3 148.1 %reduce-scatter.2.cloned.1.call-start = ((), (), s32[]{:S(2)}) async-start(), calls=%async_computation.6 | async-start | bytes 540672 | tf_op jit(solution)/shard_map/reduce_scatter | solution.py:285
Sparse Core Ops, SparseCore 0:
  287.0 143.6 all-reduce.1
  557.2 133.2 reduce-scatter.1

commit v4 on v2

v4 whole, which is shorter than its diff:
```python
import jax
import jax.numpy as jnp
from jax import lax
from jax.experimental import pallas as pl
from jax.experimental.pallas import tpu as pltpu
from jax.sharding import PartitionSpec as P

PANELS = 4
GROUP = 128
CHUNK = 1024
TOP = 32760.0
FINE = 256.0
LN2 = 0.6931471805599453
PAIRS = [(q, p) for p in range(PANELS) for q in range(p + 1, PANELS)]
VMEM_LIMIT = 56 * 1024 * 1024


def exponents(peaks):
    return jnp.ceil(jnp.log(jnp.maximum(peaks, 1e-30)) * (FINE / LN2))


def steps_of(code):
    return jnp.exp(code.astype(jnp.int32).astype(jnp.float32) * (LN2 / FINE)) * (1.0 / TOP)


def quantize(value, inverse):
    return ((value * inverse + 32768.5).astype(jnp.int32) - 32768).astype(jnp.int16)


def as_float(code):
    return code.astype(jnp.int32).astype(jnp.float32)


def encode_kernel(x_ref, code_ref):
    parts, rows, width = code_ref.shape
    length = width - GROUP

    @pl.loop(0, parts)
    def _(part):
        peaks = jnp.zeros((rows, GROUP), jnp.float32)
        for g in range(length // GROUP):
            peaks = jnp.maximum(peaks, jnp.abs(x_ref[:, lanes(part * length + g * GROUP)]))
        exponent = exponents(peaks)
        code_ref[part, :, length:] = exponent.astype(jnp.int32).astype(jnp.int16)
        inverse = jnp.exp(exponent * (-LN2 / FINE)) * TOP
        for g in range(length // GROUP):
            value = x_ref[:, lanes(part * length + g * GROUP)]
            code_ref[part, :, g * GROUP : (g + 1) * GROUP] = quantize(value, inverse)


def encode(eigvecs, parts):
    rows, columns = eigvecs.shape
    length = columns // parts
    at_once = 4 if parts % 4 == 0 else 1
    return pl.pallas_call(
        encode_kernel,
        grid=(parts // at_once,),
        in_specs=[pl.BlockSpec((rows, at_once * length), lambda i: (0, i))],
        out_specs=pl.BlockSpec((at_once, rows, length + GROUP), lambda i: (i, 0, 0)),
        out_shape=jax.ShapeDtypeStruct((parts, rows, length + GROUP), jnp.int16),
        compiler_params=pltpu.CompilerParams(vmem_limit_bytes=VMEM_LIMIT),
        cost_estimate=pl.CostEstimate(
            flops=6 * rows * columns, bytes_accessed=6 * rows * columns, transcendentals=0
        ),
        name="encode",
    )(eigvecs)


def lanes(start):
    return pl.ds(pl.multiple_of(start, GROUP), GROUP)


def decoded_chunk(code_ref, steps, i):
    return [
        as_float(code_ref[:, lanes(i * CHUNK + j * GROUP)]) * steps
        for j in range(CHUNK // GROUP)
    ]


def project_kernel(code_ref, reflector_ref, out_ref, total):
    rows, length = out_ref.shape[0], reflector_ref.shape[0]
    steps = steps_of(code_ref[:, length:])
    total[...] = jnp.zeros_like(total)

    @pl.loop(0, length // CHUNK)
    def _(i):
        value = jnp.concatenate(decoded_chunk(code_ref, steps, i), axis=1)
        high = value.astype(jnp.bfloat16)
        low = (value - high.astype(jnp.float32)).astype(jnp.bfloat16)
        block = reflector_ref[pl.ds(pl.multiple_of(i * CHUNK, CHUNK), CHUNK), :]
        total[...] += jnp.dot(
            jnp.concatenate([high, low], axis=0), block, preferred_element_type=jnp.float32
        )

    out_ref[...] = total[:rows] + total[rows:]


def project(code, reflector, rows):
    count, width = code.shape
    length, reach = reflector.shape
    return pl.pallas_call(
        project_kernel,
        grid=(count // rows,),
        in_specs=[
            pl.BlockSpec((rows, width), lambda i: (i, 0)),
            pl.BlockSpec((length, reach), lambda i: (0, 0)),
        ],
        out_specs=pl.BlockSpec((rows, reach), lambda i: (i, 0)),
        out_shape=jax.ShapeDtypeStruct((count, reach), jnp.float32),
        scratch_shapes=[pltpu.VMEM((2 * rows, reach), jnp.float32)],
        compiler_params=pltpu.CompilerParams(vmem_limit_bytes=VMEM_LIMIT),
        cost_estimate=pl.CostEstimate(
            flops=4 * count * length * reach,
            bytes_accessed=2 * count * width + 2 * length * reach,
            transcendentals=0,
        ),
        name="project",
    )(code, reflector)


def update_kernel(code_ref, coeff_ref, reflector_ref, out_ref, field, peaks):
    rows, length = field.shape
    reach = reflector_ref.shape[1]
    steps = steps_of(code_ref[:, length:])
    coeffs = jnp.concatenate([coeff_ref[:, :reach], coeff_ref[:, reach:]], axis=0)
    peaks[...] = jnp.zeros_like(peaks)

    @pl.loop(0, length // CHUNK)
    def _(i):
        block = reflector_ref[pl.ds(pl.multiple_of(i * CHUNK, CHUNK), CHUNK), :]
        change = lax.dot_general(
            coeffs, block, (((1,), (1,)), ((), ())), preferred_element_type=jnp.float32
        )
        change = change[:rows] + change[rows:]
        top = peaks[...]
        for j, part in enumerate(decoded_chunk(code_ref, steps, i)):
            new = part - change[:, j * GROUP : (j + 1) * GROUP]
            field[:, lanes(i * CHUNK + j * GROUP)] = new
            top = jnp.maximum(top, jnp.abs(new))
        peaks[...] = top

    exponent = exponents(peaks[...])
    out_ref[:, length:] = exponent.astype(jnp.int32).astype(jnp.int16)
    inverse = jnp.exp(exponent * (-LN2 / FINE)) * TOP

    @pl.loop(0, length // CHUNK)
    def _(i):
        for j in range(CHUNK // GROUP):
            at = lanes(i * CHUNK + j * GROUP)
            out_ref[:, at] = quantize(field[:, at], inverse)


def update(code, coeffs, reflector, rows):
    count, width = code.shape
    length, reach = reflector.shape
    return pl.pallas_call(
        update_kernel,
        grid=(count // rows,),
        in_specs=[
            pl.BlockSpec((rows, width), lambda i: (i, 0)),
            pl.BlockSpec((rows, 2 * reach), lambda i: (i, 0)),
            pl.BlockSpec((length, reach), lambda i: (0, 0)),
        ],
        out_specs=pl.BlockSpec((rows, width), lambda i: (i, 0)),
        out_shape=jax.ShapeDtypeStruct((count, width), jnp.int16),
        scratch_shapes=[
            pltpu.VMEM((rows, length), jnp.float32),
            pltpu.VMEM((rows, GROUP), jnp.float32),
        ],
        compiler_params=pltpu.CompilerParams(vmem_limit_bytes=VMEM_LIMIT),
        cost_estimate=pl.CostEstimate(
            flops=4 * count * length * reach,
            bytes_accessed=4 * count * width + 2 * length * reach,
            transcendentals=0,
        ),
        name="update",
    )(code, coeffs, reflector)


def decode_kernel(code_ref, out_ref):
    length = out_ref.shape[1]
    steps = steps_of(code_ref[:, length:])

    @pl.loop(0, length // CHUNK)
    def _(i):
        for j, part in enumerate(decoded_chunk(code_ref, steps, i)):
            out_ref[:, lanes(i * CHUNK + j * GROUP)] = part


def decode(code, parts):
    count, width = code.shape
    rows, length = count // parts, width - GROUP
    return pl.pallas_call(
        decode_kernel,
        grid=(parts,),
        in_specs=[pl.BlockSpec((rows, width), lambda i: (i, 0))],
        out_specs=pl.BlockSpec((rows, length), lambda i: (0, i)),
        out_shape=jax.ShapeDtypeStruct((rows, parts * length), jnp.float32),
        compiler_params=pltpu.CompilerParams(vmem_limit_bytes=VMEM_LIMIT),
        cost_estimate=pl.CostEstimate(
            flops=2 * count * length, bytes_accessed=6 * count * length, transcendentals=0
        ),
        name="decode",
    )(code)


def reflect_kernel(source_ref, shift_ref, *refs):
    pieces, reflector_ref, gram_ref = refs[:-2], refs[-2], refs[-1]
    rows, nb = pieces[0].shape
    first = pl.program_id(0) * rows
    gap = lax.broadcasted_iota(jnp.int32, (rows, nb), 0) - lax.broadcasted_iota(
        jnp.int32, (rows, nb), 1
    )
    for panel in range(PANELS):
        stored = pieces[0][...].astype(jnp.float32)
        for k in range(1, len(pieces)):
            other = pieces[k][...].astype(jnp.float32)
            stored = jnp.where(source_ref[panel] == k, other, stored)
        below = gap + (first - shift_ref[panel])
        unit = jnp.where(below == 0, 1.0, 0.0)
        block = jnp.where(below > 0, stored, unit).astype(jnp.bfloat16)
        reflector_ref[:, panel * nb : (panel + 1) * nb] = block
    block = reflector_ref[...]
    product = lax.dot_general(
        block, block, (((0,), (0,)), ((), ())), preferred_element_type=jnp.float32
    )

    @pl.when(pl.program_id(0) == 0)
    def _():
        gram_ref[...] = product

    @pl.when(pl.program_id(0) > 0)
    def _():
        gram_ref[...] += product


def reflect(pieces, source, shift):
    length, nb = pieces[0].shape
    rows, reach = min(CHUNK, length), PANELS * nb
    scalars = pl.BlockSpec(memory_space=pltpu.SMEM)
    return pl.pallas_call(
        reflect_kernel,
        grid=(length // rows,),
        in_specs=[scalars, scalars] + [pl.BlockSpec((rows, nb), lambda i: (i, 0)) for _ in pieces],
        out_specs=[
            pl.BlockSpec((rows, reach), lambda i: (i, 0)),
            pl.BlockSpec((reach, reach), lambda i: (0, 0)),
        ],
        out_shape=[
            jax.ShapeDtypeStruct((length, reach), jnp.bfloat16),
            jax.ShapeDtypeStruct((reach, reach), jnp.float32),
        ],
        compiler_params=pltpu.CompilerParams(vmem_limit_bytes=VMEM_LIMIT),
        cost_estimate=pl.CostEstimate(
            flops=2 * length * reach * reach, bytes_accessed=4 * length * reach, transcendentals=0
        ),
        name="reflect",
    )(source, shift, *pieces)


def solve_kernel(projection_ref, gram_ref, triangle_ref, out_ref):
    highest = lax.Precision.HIGHEST
    nb = triangle_ref.shape[1]
    reach = PANELS * nb
    coeffs = [None] * PANELS
    for panel in reversed(range(PANELS)):
        inner = projection_ref[:, panel * nb : (panel + 1) * nb]
        for later in range(panel + 1, PANELS):
            i, j = divmod(PAIRS.index((later, panel)), PANELS)
            block = gram_ref[i * nb : (i + 1) * nb, j * nb : (j + 1) * nb]
            inner = inner - jnp.dot(
                coeffs[later], block, precision=highest, preferred_element_type=jnp.float32
            )
        coeffs[panel] = lax.dot_general(
            inner,
            triangle_ref[panel].astype(jnp.float32),
            (((1,), (1,)), ((), ())),
            precision=highest,
            preferred_element_type=jnp.float32,
        )
        at = panel * nb
        high = coeffs[panel].astype(jnp.bfloat16)
        low = (coeffs[panel] - high.astype(jnp.float32)).astype(jnp.bfloat16)
        out_ref[:, at : at + nb] = high
        out_ref[:, reach + at : reach + at + nb] = low


def solve(projection, gram, triangles):
    count, reach = projection.shape
    return pl.pallas_call(
        solve_kernel,
        in_specs=[pl.BlockSpec(memory_space=pltpu.VMEM)] * 3,
        out_specs=pl.BlockSpec(memory_space=pltpu.VMEM),
        out_shape=jax.ShapeDtypeStruct((count, 2 * reach), jnp.bfloat16),
        compiler_params=pltpu.CompilerParams(vmem_limit_bytes=VMEM_LIMIT),
        name="solve",
    )(projection, gram, triangles)


def spread_panels(stored, n_col):
    length = stored.shape[0] // n_col
    me = lax.axis_index("col")
    pieces = []
    for k in range(n_col):
        to = lax.rem(me + k, n_col)
        piece = lax.dynamic_slice_in_dim(stored, to * length, length, axis=0)
        if k:
            piece = lax.ppermute(piece, "col", [(i, (i + k) % n_col) for i in range(n_col)])
        pieces.append(piece)
    return pieces


def local(eigvecs, panels, tfactors, owners, offsets):
    both = ("row", "col")
    n_col = lax.axis_size("col")
    n_all = lax.axis_size("row") * n_col
    me = lax.axis_index("col")
    pieces = spread_panels(panels[0], n_col)
    triangles = lax.all_gather(tfactors[0], "col")
    triangles = jnp.take(triangles, owners, axis=0)
    code = encode(eigvecs, n_all)
    code = lax.all_to_all(code, both, split_axis=0, concat_axis=0, tiled=True)
    code = code.reshape(-1, code.shape[-1])

    length, nb = pieces[0].shape
    first_row = (lax.axis_index("row") * n_col + me) * length
    reflector, gram = reflect(pieces, lax.rem(me - owners + n_col, n_col), offsets - first_row)
    blocks = [gram[q * nb : (q + 1) * nb, p * nb : (p + 1) * nb] for q, p in PAIRS]
    blocks += [jnp.zeros_like(blocks[0])] * (-len(blocks) % PANELS)
    packed = [
        jnp.concatenate(blocks[i : i + PANELS], axis=1) for i in range(0, len(blocks), PANELS)
    ]
    packed = jnp.concatenate(packed, axis=0)

    count = code.shape[0]
    rows = min(count, 256)
    projection = project(code, reflector, rows)
    own = count // n_all
    sums = jnp.concatenate(
        [projection.reshape(n_all, own, -1), packed.reshape(n_all, -1, packed.shape[1])], axis=1
    )
    sums = lax.all_to_all(sums, both, split_axis=0, concat_axis=0, tiled=True)
    sums = jnp.sum(sums, axis=0)
    sums = jnp.broadcast_to(sums[None], (n_all,) + sums.shape)
    sums = lax.all_to_all(sums, both, split_axis=0, concat_axis=0, tiled=True)
    coeffs = solve(
        sums[:, :own].reshape(projection.shape), sums[:, own:].reshape(packed.shape), triangles
    )
    code = update(code, coeffs, reflector, rows)
    code = lax.all_to_all(code, "col", split_axis=0, concat_axis=0, tiled=True)
    return decode(code, n_col)


def solution(mesh):
    in_specs = (P(("row", "col"), None), P("col", "row", None), P("col", None, None), P(), P())
    out_specs = P("col", "row")
    return jax.shard_map(local, mesh=mesh, in_specs=in_specs, out_specs=out_specs, check_vma=False)
```

time: 628 us -> 489 us (0.78)
  blocking collectives: 280 us -> 170 us
  waiting for transfers between devices: 158 us -> 202 us
  between operations: 23.4 us -> 0.14 us
  matrix products: 16.1 us -> 0 us
  Pallas kernels: 102 us -> 88 us
  other arithmetic: 13.8 us -> 2.87 us
  starting transfers between devices: 21.9 us -> 13.8 us
    ppermute x3, waiting for transfers between devices: 0.01 us -> 183 us  [spread_panels(): lax.ppermute(piece, 'col', [(i, (i + k) % n_col) for i in range(n_col)])]
    all_gather x1, blocking collectives: 178 us -> 16.9 us  [local(): triangles = lax.all_gather(tfactors[0], 'col')]
    psum x1 -> x0, waiting for transfers between devices: 105 us -> none  [local(): lax.psum(lax.dot_general(reflector, reflector, (((0,), (0,)), ((), ())),...]
    all_gather x1 -> x0, waiting for transfers between devices: 52.8 us -> none  [local(): pair = lax.all_gather(pair, both, tiled=True)]
    all_to_all x0 -> x1, blocking collectives: none -> 51.2 us  [local(): sums = lax.all_to_all(sums, both, split_axis=0, concat_axis=0, tiled=True)]
    all_to_all x1, waiting for transfers between devices: 0.01 us -> 19.2 us  [local(): sums = lax.all_to_all(sums, both, split_axis=0, concat_axis=0, tiled=True)]
    dot_general x12 -> x0, matrix products: 16.1 us -> none  [the longest x6 8.56 us: local(): inner = inner - jnp.dot(columns[later], block, precision=highest)]
    pallas_call x1, Pallas kernels: 35.7 us -> 25.4 us  [update(): pl.pallas_call(update_kernel, grid=(count // rows,), in_specs=[pl.BlockSp...]
  transfers between devices with their start and end apart: 7 -> 5, of which waited for: 2 -> 3; matrix products, arithmetic and copies ran while one was open for 6% -> 2% of each run, Pallas kernels for 4% -> 3%
where the time goes in v4:
time: 489 us; the launch traced here: 488 us
  waiting for transfers between devices  202 us (41%)
  blocking collectives  170 us (35%)
  Pallas kernels  88 us (18%)
  starting transfers between devices  13.8 us (3%)
  local copies, waits for them, and re-layouts  12 us (2%)
    ppermute x3, waiting for transfers between devices, spread_panels(): lax.ppermute(piece, 'col', [(i, (i + k) % n_col) for i in range(n_col)])  183 us
    all_to_all x1, blocking collectives, local(): code = lax.all_to_all(code, 'col', split_axis=0, concat_axis=0, tiled=True)  102 us
    all_to_all x1, blocking collectives, local(): sums = lax.all_to_all(sums, both, split_axis=0, concat_axis=0, tiled=True)  51.2 us
    pallas_call x1, Pallas kernels, update(): pl.pallas_call(update_kernel, grid=(count // rows,), in_specs=[pl.BlockSp...  25.4 us
    all_to_all x1, waiting for transfers between devices, local(): sums = lax.all_to_all(sums, both, split_axis=0, concat_axis=0, tiled=True)  19.2 us
    pallas_call x1, Pallas kernels, project(): pl.pallas_call(project_kernel, grid=(count // rows,), in_specs=[pl.BlockS...  17.4 us
    all_gather x1, blocking collectives, local(): triangles = lax.all_gather(tfactors[0], 'col')  16.9 us
    pallas_call x1, Pallas kernels, reflect(): pl.pallas_call(reflect_kernel, grid=(length // rows,), in_specs=[scalars,...  14.3 us
  transfers between devices with their start and end apart: 5, of which 3 were waited for; matrix products, arithmetic and copies ran while one was open for 2% of the time, Pallas kernels for 3%

profile of v4, /device:TPU:0, one launch (start us, length us, event | category | flops | bytes accessed | tf_op | source)
XLA Modules:
  0.0 488.5 jit_solution(10672391908347565742)
XLA Ops:
  0.0 13.8 %encode.1 = s16[32,16,8320]{2,1,0:T(8,128)(2,1)} custom-call(f32[16,262144]{1,0:T(8,128)} %x_ref.1), custom_call_target="tpu_custom_call" | custom-call | flops 25165824 | bytes 25165824 | tf_op jit(solution)/shard_map/encode/pallas_call | solution.py:55
  13.8 7.4 %all-to-all-start = ((s16[32,16,8320]{2,1,0:T(8,128)(2,1)}), s16[32,16,8320]{2,1,0:T(8,128)(2,1)}, u32[]{:S(2)}, u32[]{:S(2)}) async-start(s16[32,16,8320]{2,1,0:T(8,128)(2,1)} %encode.1), calls=%async_computation | async-start | bytes 17039360 | tf_op jit(solution)/shard_map/all_to_all | solution.py:322
  21.2 0.0 copy-start.1
  21.3 0.0 copy-start.2
  21.3 6.2 %dynamic-slice_bitcast_fusion = (bf16[8192,128]{1,0:T(8,128)(2,1)}, bf16[8192,128]{1,0:T(8,128)(2,1)}, bf16[8192,128]{1,0:T(8,128)(2,1)}, bf16[8192,128]{1,0:T(8,128)(2,1)S(1)}) fusion(bf16[1,32768,128]{2,1,0:T(8,128)(2,1)} %param.6, s32[]{:T(128)S(6)} %select_n.24, s32[]{:T(128)S(6)} %select_n.22, s32[]{:T(128)S(6)} %select_n.21, s32[]{:T(128)S(6)} %select_n.23), kind=kLoop, calls=%fused_computation.1 | loop fusion | bytes 16777232 | tf_op jit(solution)/shard_map/dynamic_slice | solution.py:306
  27.5 2.6 collective-permute-start.2
  30.1 0.0 collective-permute-start
  30.1 1.1 collective-permute-start.1
  31.2 0.0 copy-done.1
  31.2 0.0 copy-done.2
  31.2 0.6 compare_select_fusion
  31.8 126.5 %collective-permute-done.2.refs_3_ = bf16[8192,128]{1,0:T(8,128)(2,1)} collective-permute-done((bf16[8192,128]{1,0:T(8,128)(2,1)}, bf16[8192,128]{1,0:T(8,128)(2,1)}, u32[]{:S(2)}, u32[]{:S(2)}) %collective-permute-start.2) | collective-permute-done | bytes 2097184 | tf_op jit(solution)/shard_map/ppermute | solution.py:308
  158.3 56.1 %collective-permute-done.refs_1_ = bf16[8192,128]{1,0:T(8,128)(2,1)} collective-permute-done((bf16[8192,128]{1,0:T(8,128)(2,1)}, bf16[8192,128]{1,0:T(8,128)(2,1)}, u32[]{:S(2)}, u32[]{:S(2)}) %collective-permute-start) | collective-permute-done | bytes 2097184 | tf_op jit(solution)/shard_map/ppermute | solution.py:308
  214.4 0.0 collective-permute-done.1.refs_2_
  214.4 14.3 %reflect.1 = (bf16[8192,512]{1,0:T(8,128)(2,1)}, f32[512,512]{1,0:T(8,128)}) custom-call(s32[4]{0:T(128)} %get-tuple-element.18.source_ref, s32[4]{0:T(128)} %get-tuple-element.19.shift_ref, bf16[8192,128]{1,0:T(8,128)(2,1)} %get-tuple-element.11.refs_0_, bf16[8192,128]{1,0:T(8,128)(2,1)} %collective-permute-done.refs_1_, ...), custom_call_target="tpu_custom_call" | custom-call | flops 4294967296 | bytes 16777216 | tf_op jit(solution)/shard_map/reflect/pallas_call | solution.py:241
  228.7 0.9 slice.27
  229.6 1.0 fusion.2
  230.7 0.0 all-to-all-done
  230.7 17.4 %project.1 = f32[512,512]{1,0:T(8,128)} custom-call(s16[512,8320]{1,0:T(8,128)(2,1)} %bitcast.code_ref, bf16[8192,512]{1,0:T(8,128)(2,1)} %get-tuple-element.7.reflector_ref), custom_call_target="tpu_custom_call" | custom-call | flops 8589934592 | bytes 16908288 | tf_op jit(solution)/shard_map/project/pallas_call | solution.py:101
  248.0 1.4 pad_maximum_fusion
  249.4 51.2 %all_to_all.26 = f32[32,24,512]{2,1,0:T(8,128)S(1)} all-to-all(f32[32,24,512]{2,1,0:T(8,128)S(1)} %pad_maximum_fusion), channel_id=1, replica_groups=mesh['row'=8,'col'=4] {'row','col'}, dimensions={0} | all-to-all | bytes 3145728 | tf_op jit(solution)/shard_map/all_to_all | solution.py:342
  300.6 0.1 reduce_sum.9
  300.7 0.0 copy-start
  300.7 1.3 broadcast_in_dim.18
  302.0 2.7 all-to-all-start.2
  304.7 0.0 copy-done
  304.7 16.9 %all_gather.3 = bf16[4,128,128]{2,1,0:T(8,128)(2,1)S(1)} all-gather(bf16[1,128,128]{2,1,0:T(8,128)(2,1)S(1)} %copy-done), channel_id=1, replica_groups=mesh['row'=8,'col'=4] {'col'}, dimensions={0}, use_global_device_ids=true | all-gather | bytes 163840 | tf_op jit(solution)/shard_map/all_gather | solution.py:319
  321.7 0.6 gather_fusion
  322.3 0.7 broadcast_select_fusion.triangle_ref
  323.0 19.2 %all-to-all-done.2 = f32[32,24,512]{2,1,0:T(8,128)S(1)} async-done(((f32[32,24,512]{2,1,0:T(8,128)}), f32[32,24,512]{2,1,0:T(8,128)S(1)}, u32[]{:S(2)}, u32[]{:S(2)}) %all-to-all-start.2) | async-done | bytes 1572896 | tf_op jit(solution)/shard_map/all_to_all | solution.py:345
  342.2 0.9 slice_bitcast_fusion.gram_ref
  343.0 1.1 slice.32
  344.1 6.2 %solve.1.coeff_ref = bf16[512,1024]{1,0:T(8,128)(2,1)} custom-call(f32[512,512]{1,0:T(8,128)} %bitcast.19, f32[256,512]{1,0:T(8,128)} %slice_bitcast_fusion.gram_ref, bf16[4,128,128]{2,1,0:T(8,128)(2,1)} %broadcast_select_fusion.triangle_ref), custom_call_target="tpu_custom_call" | custom-call | tf_op jit(solution)/shard_map/solve/pallas_call | solution.py:290
  350.3 25.4 %update.1 = s16[512,8320]{1,0:T(8,128)(2,1)} custom-call(s16[512,8320]{1,0:T(8,128)(2,1)} %bitcast.code_ref, bf16[512,1024]{1,0:T(8,128)(2,1)} %solve.1.coeff_ref, bf16[8192,512]{1,0:T(8,128)(2,1)} %get-tuple-element.7.reflector_ref), custom_call_target="tpu_custom_call" | custom-call | flops 8589934592 | bytes 25427968 | tf_op jit(solution)/shard_map/update/pallas_call | solution.py:156
  375.7 101.9 %all_to_all.27 = s16[4,128,8320]{2,1,0:T(8,128)(2,1)} all-to-all(s16[4,128,8320]{2,1,0:T(8,128)(2,1)} %bitcast.18), channel_id=1, replica_groups=mesh['row'=8,'col'=4] {'col'}, dimensions={0} | all-to-all | bytes 17039360 | tf_op jit(solution)/shard_map/all_to_all | solution.py:350
  477.6 10.9 %decode.1 = f32[128,32768]{1,0:T(8,128)} custom-call(s16[512,8320]{1,0:T(8,128)(2,1)} %bitcast.17), custom_call_target="tpu_custom_call" | custom-call | flops 8388608 | bytes 25165824 | tf_op jit(solution)/shard_map/decode/pallas_call | solution.py:193
  (3 shorter events, 0.1 us)
Async XLA Ops:
  13.8 216.9 %all-to-all-start = ((s16[32,16,8320]{2,1,0:T(8,128)(2,1)}), s16[32,16,8320]{2,1,0:T(8,128)(2,1)}, u32[]{:S(2)}, u32[]{:S(2)}) async-start(s16[32,16,8320]{2,1,0:T(8,128)(2,1)} %encode.1), calls=%async_computation | async-start | bytes 17039360 | tf_op jit(solution)/shard_map/all_to_all | solution.py:322
  21.2 10.0 %copy-start.1 = (s32[4]{0:T(128)S(1)}, s32[4]{0:T(128)}, u32[]{:S(2)}) copy-start(s32[4]{0:T(128)} %param.9) | copy-start | bytes 52
  21.3 10.0 %copy-start.2 = (s32[4]{0:T(128)S(1)}, s32[4]{0:T(128)}, u32[]{:S(2)}) copy-start(s32[4]{0:T(128)} %param.8) | copy-start | bytes 52
  27.5 130.8 %collective-permute-start.2 = (bf16[8192,128]{1,0:T(8,128)(2,1)}, bf16[8192,128]{1,0:T(8,128)(2,1)}, u32[]{:S(2)}, u32[]{:S(2)}) collective-permute-start(bf16[8192,128]{1,0:T(8,128)(2,1)} %get-tuple-element.9), channel_id=1, source_target_pairs={{0,3},{1,0},{2,1},{3,2},{4,7},{5,4},{6,5},{7,6},{8,11},{9,8},{10,9... | collective-permute-start | bytes 6291464 | tf_op jit(solution)/shard_map/ppermute | solution.py:308
  30.1 184.3 %collective-permute-start = (bf16[8192,128]{1,0:T(8,128)(2,1)}, bf16[8192,128]{1,0:T(8,128)(2,1)}, u32[]{:S(2)}, u32[]{:S(2)}) collective-permute-start(bf16[8192,128]{1,0:T(8,128)(2,1)} %get-tuple-element.10), channel_id=1, source_target_pairs={{0,1},{1,2},{2,3},{3,0},{4,5},{5,6},{6,7},{7,4},{8,9},{9,10},{10,1... | collective-permute-start | bytes 6291464 | tf_op jit(solution)/shard_map/ppermute | solution.py:308
  30.1 184.3 %collective-permute-start.1 = (bf16[8192,128]{1,0:T(8,128)(2,1)S(1)}, bf16[8192,128]{1,0:T(8,128)(2,1)}, u32[]{:S(2)}, u32[]{:S(2)}) collective-permute-start(bf16[8192,128]{1,0:T(8,128)(2,1)S(1)} %get-tuple-element.12), channel_id=1, source_target_pairs={{0,2},{1,3},{2,0},{3,1},{4,6},{5,7},{6,4},{7,5},{8,10},{9,11},{10,... | collective-permute-start | bytes 6291464 | tf_op jit(solution)/shard_map/ppermute | solution.py:308
  300.7 4.0 copy-start
  302.0 40.1 %all-to-all-start.2 = ((f32[32,24,512]{2,1,0:T(8,128)}), f32[32,24,512]{2,1,0:T(8,128)S(1)}, u32[]{:S(2)}, u32[]{:S(2)}) async-start(f32[32,24,512]{2,1,0:T(8,128)} %broadcast_in_dim.18), calls=%async_computation.2 | async-start | bytes 3145728 | tf_op jit(solution)/shard_map/all_to_all | solution.py:345

commit v5 on v4

--- a/solution.py
+++ b/solution.py
@@ -121,8 +121,14 @@
 def update_kernel(code_ref, coeff_ref, reflector_ref, out_ref, field, peaks):
     rows, length = field.shape
     reach = reflector_ref.shape[1]
-    steps = steps_of(code_ref[:, length:])
-    coeffs = jnp.concatenate([coeff_ref[:, :reach], coeff_ref[:, reach:]], axis=0)
+
+    def joined(value):
+        return value.reshape(rows, value.shape[-1])
+
+    steps = joined(steps_of(code_ref[:, :, length:]))
+    coeffs = jnp.concatenate(
+        [joined(coeff_ref[:, :, :reach]), joined(coeff_ref[:, :, reach:])], axis=0
+    )
     peaks[...] = jnp.zeros_like(peaks)
 
     @pl.loop(0, length // CHUNK)
@@ -133,39 +139,44 @@
         )
         change = change[:rows] + change[rows:]
         top = peaks[...]
-        for j, part in enumerate(decoded_chunk(code_ref, steps, i)):
+        for j in range(CHUNK // GROUP):
+            at = lanes(i * CHUNK + j * GROUP)
+            part = joined(as_float(code_ref[:, :, at])) * steps
             new = part - change[:, j * GROUP : (j + 1) * GROUP]
-            field[:, lanes(i * CHUNK + j * GROUP)] = new
+            field[:, at] = new
             top = jnp.maximum(top, jnp.abs(new))
         peaks[...] = top
 
     exponent = exponents(peaks[...])
-    out_ref[:, length:] = exponent.astype(jnp.int32).astype(jnp.int16)
+    split = out_ref.shape[:2] + (GROUP,)
+    out_ref[:, :, length:] = exponent.reshape(split).astype(jnp.int32).astype(jnp.int16)
     inverse = jnp.exp(exponent * (-LN2 / FINE)) * TOP
 
     @pl.loop(0, length // CHUNK)
     def _(i):
         for j in range(CHUNK // GROUP):
             at = lanes(i * CHUNK + j * GROUP)
-            out_ref[:, at] = quantize(field[:, at], inverse)
-
-
-def update(code, coeffs, reflector, rows):
-    count, width = code.shape
+            value = field[:, at].reshape(split)
+            out_ref[:, :, at] = quantize(value, inverse.reshape(split))
+
+
+def update(code, coeffs, reflector, half):
+    parts, _, rows, width = code.shape
     length, reach = reflector.shape
+    count = parts * rows
     return pl.pallas_call(
         update_kernel,
-        grid=(count // rows,),
+        grid=(1,),
         in_specs=[
-            pl.BlockSpec((rows, width), lambda i: (i, 0)),
-            pl.BlockSpec((rows, 2 * reach), lambda i: (i, 0)),
+            pl.BlockSpec((parts, None, rows, width), lambda i: (0, half, 0, 0)),
+            pl.BlockSpec((parts, None, rows, 2 * reach), lambda i: (0, half, 0, 0)),
             pl.BlockSpec((length, reach), lambda i: (0, 0)),
         ],
-        out_specs=pl.BlockSpec((rows, width), lambda i: (i, 0)),
-        out_shape=jax.ShapeDtypeStruct((count, width), jnp.int16),
+        out_specs=pl.BlockSpec((parts, rows, width), lambda i: (0, 0, 0)),
+        out_shape=jax.ShapeDtypeStruct((parts, rows, width), jnp.int16),
         scratch_shapes=[
-            pltpu.VMEM((rows, length), jnp.float32),
-            pltpu.VMEM((rows, GROUP), jnp.float32),
+            pltpu.VMEM((count, length), jnp.float32),
+            pltpu.VMEM((count, GROUP), jnp.float32),
         ],
         compiler_params=pltpu.CompilerParams(vmem_limit_bytes=VMEM_LIMIT),
         cost_estimate=pl.CostEstimate(
@@ -177,7 +188,8 @@
     )(code, coeffs, reflector)
 
 
-def decode_kernel(code_ref, out_ref):
+def decode_kernel(code_ref, *refs):
+    out_ref = refs[-1]
     length = out_ref.shape[1]
     steps = steps_of(code_ref[:, length:])
 
@@ -187,21 +199,26 @@
             out_ref[:, lanes(i * CHUNK + j * GROUP)] = part
 
 
-def decode(code, parts):
-    count, width = code.shape
-    rows, length = count // parts, width - GROUP
+def decode(code, before, half):
+    parts, rows, width = code.shape
+    length = width - GROUP
+    again = [] if before is None else [before]
     return pl.pallas_call(
         decode_kernel,
         grid=(parts,),
-        in_specs=[pl.BlockSpec((rows, width), lambda i: (i, 0))],
-        out_specs=pl.BlockSpec((rows, length), lambda i: (0, i)),
-        out_shape=jax.ShapeDtypeStruct((rows, parts * length), jnp.float32),
-        compiler_params=pltpu.CompilerParams(vmem_limit_bytes=VMEM_LIMIT),
-        cost_estimate=pl.CostEstimate(
-            flops=2 * count * length, bytes_accessed=6 * count * length, transcendentals=0
+        in_specs=[pl.BlockSpec((None, rows, width), lambda i: (i, 0, 0))]
+        + [pl.BlockSpec(memory_space=pl.ANY) for _ in again],
+        out_specs=pl.BlockSpec((rows, length), lambda i: (half, i)),
+        out_shape=jax.ShapeDtypeStruct((2 * rows, parts * length), jnp.float32),
+        input_output_aliases={1: 0} if again else {},
+        compiler_params=pltpu.CompilerParams(vmem_limit_bytes=VMEM_LIMIT),
+        cost_estimate=pl.CostEstimate(
+            flops=2 * parts * rows * length,
+            bytes_accessed=6 * parts * rows * length,
+            transcendentals=0,
         ),
         name="decode",
-    )(code)
+    )(code, *again)
 
 
 def reflect_kernel(source_ref, shift_ref, *refs):
@@ -297,17 +314,21 @@
     )(projection, gram, triangles)
 
 
-def spread_panels(stored, n_col):
+def cut_panels(stored, n_col):
     length = stored.shape[0] // n_col
     me = lax.axis_index("col")
-    pieces = []
-    for k in range(n_col):
-        to = lax.rem(me + k, n_col)
-        piece = lax.dynamic_slice_in_dim(stored, to * length, length, axis=0)
-        if k:
-            piece = lax.ppermute(piece, "col", [(i, (i + k) % n_col) for i in range(n_col)])
-        pieces.append(piece)
-    return pieces
+    return [
+        lax.dynamic_slice_in_dim(stored, lax.rem(me + k, n_col) * length, length, axis=0)
+        for k in range(n_col)
+    ]
+
+
+def spread_panels(pieces):
+    n = len(pieces)
+    return [
+        lax.ppermute(piece, "col", [(i, (i + k) % n) for i in range(n)]) if k else piece
+        for k, piece in enumerate(pieces)
+    ]
 
 
 def local(eigvecs, panels, tfactors, owners, offsets):
@@ -315,7 +336,8 @@
     n_col = lax.axis_size("col")
     n_all = lax.axis_size("row") * n_col
     me = lax.axis_index("col")
-    pieces = spread_panels(panels[0], n_col)
+    pieces, eigvecs = lax.optimization_barrier((cut_panels(panels[0], n_col), eigvecs))
+    pieces = spread_panels(pieces)
     triangles = lax.all_gather(tfactors[0], "col")
     triangles = jnp.take(triangles, owners, axis=0)
     code = encode(eigvecs, n_all)
@@ -346,9 +368,14 @@
     coeffs = solve(
         sums[:, :own].reshape(projection.shape), sums[:, own:].reshape(packed.shape), triangles
     )
-    code = update(code, coeffs, reflector, rows)
-    code = lax.all_to_all(code, "col", split_axis=0, concat_axis=0, tiled=True)
-    return decode(code, n_col)
+    split = (n_col, 2, count // (2 * n_col), -1)
+    code, coeffs = code.reshape(split), coeffs.reshape(split)
+    back = None
+    for half in range(2):
+        part = update(code, coeffs, reflector, half)
+        part = lax.all_to_all(part, "col", split_axis=0, concat_axis=0, tiled=True)
+        back = decode(part, back, half)
+    return back
 
 
 def solution(mesh):

time: 489 us -> 485 us (level)
  blocking collectives: 170 us -> 66.6 us
  waiting for transfers between devices: 202 us -> 281 us
  starting transfers between devices: 13.8 us -> 24.5 us
  Pallas kernels: 88 us -> 96.7 us
    all_to_all x1 -> x0, blocking collectives: 102 us -> none  [local(): code = lax.all_to_all(code, 'col', split_axis=0, concat_axis=0, tiled=True)]
    all_to_all x0 -> x2, waiting for transfers between devices: none -> 74 us  [local(): part = lax.all_to_all(part, 'col', split_axis=0, concat_axis=0, tiled=True)]
    all_to_all x0 -> x2, starting transfers between devices: none -> 9.72 us  [local(): part = lax.all_to_all(part, 'col', split_axis=0, concat_axis=0, tiled=True)]
    pallas_call x2 -> x4, Pallas kernels: 36.3 us -> 45 us  [the longest x2 32.1 us: update(): pl.pallas_call(update_kernel, grid=(1,), in_specs=[pl.BlockSpec((parts, N...]
    ppermute x3, waiting for transfers between devices: 183 us -> 188 us  [spread_panels(): lax.ppermute(piece, 'col', [(i, (i + k) % n) for i in range(n)])]
  transfers between devices with their start and end apart: 5 -> 7, of which waited for: 3 -> 6; matrix products, arithmetic and copies ran while one was open for 2% -> 1% of each run, Pallas kernels for 3% -> 8%
where the time goes in v5:
time: 485 us; the launch traced here: 484 us
  waiting for transfers between devices  281 us (58%)
  Pallas kernels  96.7 us (20%)
  blocking collectives  66.6 us (14%)
  starting transfers between devices  24.5 us (5%)
  local copies, waits for them, and re-layouts  11.9 us (2%)
    ppermute x3, waiting for transfers between devices, spread_panels(): lax.ppermute(piece, 'col', [(i, (i + k) % n) for i in range(n)])  188 us
    all_to_all x2, waiting for transfers between devices, local(): part = lax.all_to_all(part, 'col', split_axis=0, concat_axis=0, tiled=True)  74 us
    all_to_all x1, blocking collectives, local(): sums = lax.all_to_all(sums, both, split_axis=0, concat_axis=0, tiled=True)  49.6 us
    pallas_call x2, Pallas kernels, update(): pl.pallas_call(update_kernel, grid=(1,), in_specs=[pl.BlockSpec((parts, N...  32.1 us
    all_to_all x1, waiting for transfers between devices, local(): sums = lax.all_to_all(sums, both, split_axis=0, concat_axis=0, tiled=True)  19.2 us
    pallas_call x1, Pallas kernels, project(): pl.pallas_call(project_kernel, grid=(count // rows,), in_specs=[pl.BlockS...  17.4 us
    all_gather x1, blocking collectives, local(): triangles = lax.all_gather(tfactors[0], 'col')  16.9 us
    pallas_call x1, Pallas kernels, reflect(): pl.pallas_call(reflect_kernel, grid=(length // rows,), in_specs=[scalars,...  14.3 us
  transfers between devices with their start and end apart: 7, of which 6 were waited for; matrix products, arithmetic and copies ran while one was open for 1% of the time, Pallas kernels for 8%

profile of v5, /device:TPU:0, one launch (start us, length us, event | category | flops | bytes accessed | tf_op | source)
XLA Modules:
  0.0 483.8 jit_solution(17613070748815503094)
XLA Ops:
  0.0 6.2 %dynamic-slice_bitcast_fusion = (bf16[8192,128]{1,0:T(8,128)(2,1)S(1)}, bf16[8192,128]{1,0:T(8,128)(2,1)}, bf16[8192,128]{1,0:T(8,128)(2,1)}, bf16[8192,128]{1,0:T(8,128)(2,1)}) fusion(bf16[1,32768,128]{2,1,0:T(8,128)(2,1)} %param.6, s32[]{:T(128)S(6)} %select_n.24, s32[]{:T(128)S(6)} %select_n.22, s32[]{:T(128)S(6)} %select_n.21, s32[]{:T(128)S(6)} %select_n.23), kind=kLoop, calls=%fused_computation.1 | loop fusion | bytes 16777232 | tf_op jit(solution)/shard_map/dynamic_slice | solution.py:321
  6.2 13.8 %encode.1 = s16[32,16,8320]{2,1,0:T(8,128)(2,1)} custom-call(f32[16,262144]{1,0:T(8,128)} %x_ref), custom_call_target="tpu_custom_call" | custom-call | flops 25165824 | bytes 25165824 | tf_op jit(solution)/shard_map/encode/pallas_call | solution.py:55
  20.0 0.0 copy-start.1
  20.0 0.0 copy-start.2
  20.0 7.4 %all-to-all-start = ((s16[32,16,8320]{2,1,0:T(8,128)(2,1)}), s16[32,16,8320]{2,1,0:T(8,128)(2,1)}, u32[]{:S(2)}, u32[]{:S(2)}) async-start(s16[32,16,8320]{2,1,0:T(8,128)(2,1)} %encode.1), calls=%async_computation | async-start | bytes 17039360 | tf_op jit(solution)/shard_map/all_to_all | solution.py:344
  27.4 1.8 collective-permute-start
  29.2 1.5 collective-permute-start.1
  30.6 1.5 collective-permute-start.2
  32.1 0.0 copy-done.1
  32.1 0.0 copy-done.2
  32.1 0.5 compare_select_fusion
  32.7 135.8 %collective-permute-done.refs_1_ = bf16[8192,128]{1,0:T(8,128)(2,1)} collective-permute-done((bf16[8192,128]{1,0:T(8,128)(2,1)}, bf16[8192,128]{1,0:T(8,128)(2,1)}, u32[]{:S(2)}, u32[]{:S(2)}) %collective-permute-start) | collective-permute-done | bytes 2097184 | tf_op jit(solution)/shard_map/ppermute | solution.py:329
  168.4 43.0 %collective-permute-done.1.refs_2_ = bf16[8192,128]{1,0:T(8,128)(2,1)} collective-permute-done((bf16[8192,128]{1,0:T(8,128)(2,1)}, bf16[8192,128]{1,0:T(8,128)(2,1)}, u32[]{:S(2)}, u32[]{:S(2)}) %collective-permute-start.1) | collective-permute-done | bytes 2097184 | tf_op jit(solution)/shard_map/ppermute | solution.py:329
  211.5 9.2 %collective-permute-done.2.refs_3_ = bf16[8192,128]{1,0:T(8,128)(2,1)} collective-permute-done((bf16[8192,128]{1,0:T(8,128)(2,1)S(1)}, bf16[8192,128]{1,0:T(8,128)(2,1)}, u32[]{:S(2)}, u32[]{:S(2)}) %collective-permute-start.2) | collective-permute-done | bytes 2097184 | tf_op jit(solution)/shard_map/ppermute | solution.py:329
  220.7 14.3 %reflect.1 = (bf16[8192,512]{1,0:T(8,128)(2,1)}, f32[512,512]{1,0:T(8,128)}) custom-call(s32[4]{0:T(128)} %get-tuple-element.28.source_ref, s32[4]{0:T(128)} %get-tuple-element.29.shift_ref, bf16[8192,128]{1,0:T(8,128)(2,1)} %get-tuple-element.13.refs_0_, bf16[8192,128]{1,0:T(8,128)(2,1)} %collective-permute-done.refs_1_, ...), custom_call_target="tpu_custom_call" | custom-call | flops 4294967296 | bytes 16777216 | tf_op jit(solution)/shard_map/reflect/pallas_call | solution.py:258
  235.0 0.9 slice.27
  235.9 1.0 fusion.2
  236.9 0.0 all-to-all-done
  236.9 17.4 %project.1 = f32[512,512]{1,0:T(8,128)} custom-call(s16[512,8320]{1,0:T(8,128)(2,1)} %bitcast.5.code_ref, bf16[8192,512]{1,0:T(8,128)(2,1)} %get-tuple-element.17.reflector_ref), custom_call_target="tpu_custom_call" | custom-call | flops 8589934592 | bytes 16908288 | tf_op jit(solution)/shard_map/project/pallas_call | solution.py:101
  254.3 1.4 pad_maximum_fusion
  255.7 49.6 %all_to_all.25 = f32[32,24,512]{2,1,0:T(8,128)S(1)} all-to-all(f32[32,24,512]{2,1,0:T(8,128)S(1)} %pad_maximum_fusion), channel_id=1, replica_groups=mesh['row'=8,'col'=4] {'row','col'}, dimensions={0} | all-to-all | bytes 3145728 | tf_op jit(solution)/shard_map/all_to_all | solution.py:364
  305.3 0.1 reduce_sum.9
  305.4 0.0 copy-start
  305.4 1.3 broadcast_in_dim.18
  306.8 2.7 all-to-all-start.2
  309.5 0.0 copy-done
  309.5 16.9 %all_gather.3 = bf16[4,128,128]{2,1,0:T(8,128)(2,1)S(1)} all-gather(bf16[1,128,128]{2,1,0:T(8,128)(2,1)S(1)} %copy-done), channel_id=1, replica_groups=mesh['row'=8,'col'=4] {'col'}, dimensions={0}, use_global_device_ids=true | all-gather | bytes 163840 | tf_op jit(solution)/shard_map/all_gather | solution.py:341
  326.4 0.6 gather_fusion
  327.0 0.7 broadcast_select_fusion.triangle_ref
  327.8 19.2 %all-to-all-done.2 = f32[32,24,512]{2,1,0:T(8,128)S(1)} async-done(((f32[32,24,512]{2,1,0:T(8,128)}), f32[32,24,512]{2,1,0:T(8,128)S(1)}, u32[]{:S(2)}, u32[]{:S(2)}) %all-to-all-start.2) | async-done | bytes 1572896 | tf_op jit(solution)/shard_map/all_to_all | solution.py:367
  346.9 0.8 slice_bitcast_fusion.gram_ref
  347.8 1.1 slice.32
  348.8 6.2 %solve.1 = bf16[512,1024]{1,0:T(8,128)(2,1)} custom-call(f32[512,512]{1,0:T(8,128)} %bitcast.19, f32[256,512]{1,0:T(8,128)} %slice_bitcast_fusion.gram_ref, bf16[4,128,128]{2,1,0:T(8,128)(2,1)} %broadcast_select_fusion.triangle_ref), custom_call_target="tpu_custom_call" | custom-call | tf_op jit(solution)/shard_map/solve/pallas_call | solution.py:307
  355.0 16.1 %update.3 = s16[4,64,8320]{2,1,0:T(8,128)(2,1)} custom-call(s16[4,2,64,8320]{3,2,1,0:T(8,128)(2,1)} %bitcast.4.code_ref, bf16[4,2,64,1024]{3,2,1,0:T(8,128)(2,1)} %bitcast.17, bf16[8192,512]{1,0:T(8,128)(2,1)} %get-tuple-element.17.reflector_ref), custom_call_target="tpu_custom_call" | custom-call | flops 4294967296 | bytes 16908288 | tf_op jit(solution)/shard_map/update/pallas_call | solution.py:167
  371.1 4.9 %all-to-all-start.4 = ((s16[4,64,8320]{2,1,0:T(8,128)(2,1)}), s16[4,64,8320]{2,1,0:T(8,128)(2,1)}, u32[]{:S(2)}, u32[]{:S(2)}) async-start(s16[4,64,8320]{2,1,0:T(8,128)(2,1)} %update.3), calls=%async_computation.4 | async-start | bytes 8519680 | tf_op jit(solution)/shard_map/all_to_all | solution.py:376
  376.0 16.1 %update.2 = s16[4,64,8320]{2,1,0:T(8,128)(2,1)} custom-call(s16[4,2,64,8320]{3,2,1,0:T(8,128)(2,1)} %bitcast.4.code_ref, bf16[4,2,64,1024]{3,2,1,0:T(8,128)(2,1)} %bitcast.18, bf16[8192,512]{1,0:T(8,128)(2,1)} %get-tuple-element.17.reflector_ref), custom_call_target="tpu_custom_call" | custom-call | flops 4294967296 | bytes 16908288 | tf_op jit(solution)/shard_map/update/pallas_call | solution.py:167
  392.0 32.4 %all-to-all-done.4.code_ref = s16[4,64,8320]{2,1,0:T(8,128)(2,1)} async-done(((s16[4,64,8320]{2,1,0:T(8,128)(2,1)}), s16[4,64,8320]{2,1,0:T(8,128)(2,1)}, u32[]{:S(2)}, u32[]{:S(2)}) %all-to-all-start.4) | async-done | bytes 4259872 | tf_op jit(solution)/shard_map/all_to_all | solution.py:376
  424.5 4.9 %all-to-all-start.3 = ((s16[4,64,8320]{2,1,0:T(8,128)(2,1)}), s16[4,64,8320]{2,1,0:T(8,128)(2,1)}, u32[]{:S(2)}, u32[]{:S(2)}) async-start(s16[4,64,8320]{2,1,0:T(8,128)(2,1)} %update.2), calls=%async_computation.3 | async-start | bytes 8519680 | tf_op jit(solution)/shard_map/all_to_all | solution.py:376
  429.3 6.4 %decode.2.refs_0_ = f32[128,32768]{1,0:T(8,128)} custom-call(s16[4,64,8320]{2,1,0:T(8,128)(2,1)} %all-to-all-done.4.code_ref), custom_call_target="tpu_custom_call" | custom-call | flops 4194304 | bytes 12582912 | tf_op jit(solution)/shard_map/decode/pallas_call | solution.py:206
  435.8 41.6 %all-to-all-done.3.code_ref = s16[4,64,8320]{2,1,0:T(8,128)(2,1)} async-done(((s16[4,64,8320]{2,1,0:T(8,128)(2,1)}), s16[4,64,8320]{2,1,0:T(8,128)(2,1)}, u32[]{:S(2)}, u32[]{:S(2)}) %all-to-all-start.3) | async-done | bytes 4259872 | tf_op jit(solution)/shard_map/all_to_all | solution.py:376
  477.4 6.4 %decode.3 = f32[128,32768]{1,0:T(8,128)} custom-call(s16[4,64,8320]{2,1,0:T(8,128)(2,1)} %all-to-all-done.3.code_ref, f32[128,32768]{1,0:T(8,128)} %decode.2.refs_0_), custom_call_target="tpu_custom_call", output_to_operand_aliasing={{}: (1, {})} | custom-call | flops 4194304 | bytes 12582912 | tf_op jit(solution)/shard_map/decode/pallas_call | solution.py:206
  (3 shorter events, 0.1 us)
Async XLA Ops:
  20.0 12.1 %copy-start.1 = (s32[4]{0:T(128)S(1)}, s32[4]{0:T(128)}, u32[]{:S(2)}) copy-start(s32[4]{0:T(128)} %param.9) | copy-start | bytes 52
  20.0 12.1 %copy-start.2 = (s32[4]{0:T(128)S(1)}, s32[4]{0:T(128)}, u32[]{:S(2)}) copy-start(s32[4]{0:T(128)} %param.8) | copy-start | bytes 52
  20.0 216.9 %all-to-all-start = ((s16[32,16,8320]{2,1,0:T(8,128)(2,1)}), s16[32,16,8320]{2,1,0:T(8,128)(2,1)}, u32[]{:S(2)}, u32[]{:S(2)}) async-start(s16[32,16,8320]{2,1,0:T(8,128)(2,1)} %encode.1), calls=%async_computation | async-start | bytes 17039360 | tf_op jit(solution)/shard_map/all_to_all | solution.py:344
  27.4 141.0 %collective-permute-start = (bf16[8192,128]{1,0:T(8,128)(2,1)}, bf16[8192,128]{1,0:T(8,128)(2,1)}, u32[]{:S(2)}, u32[]{:S(2)}) collective-permute-start(bf16[8192,128]{1,0:T(8,128)(2,1)} %get-tuple-element.14), channel_id=1, source_target_pairs={{0,1},{1,2},{2,3},{3,0},{4,5},{5,6},{6,7},{7,4},{8,9},{9,10},{10,1... | collective-permute-start | bytes 6291464 | tf_op jit(solution)/shard_map/ppermute | solution.py:329
  29.2 182.3 %collective-permute-start.1 = (bf16[8192,128]{1,0:T(8,128)(2,1)}, bf16[8192,128]{1,0:T(8,128)(2,1)}, u32[]{:S(2)}, u32[]{:S(2)}) collective-permute-start(bf16[8192,128]{1,0:T(8,128)(2,1)} %get-tuple-element.15), channel_id=1, source_target_pairs={{0,2},{1,3},{2,0},{3,1},{4,6},{5,7},{6,4},{7,5},{8,10},{9,11},{10,... | collective-permute-start | bytes 6291464 | tf_op jit(solution)/shard_map/ppermute | solution.py:329
  30.6 190.0 %collective-permute-start.2 = (bf16[8192,128]{1,0:T(8,128)(2,1)S(1)}, bf16[8192,128]{1,0:T(8,128)(2,1)}, u32[]{:S(2)}, u32[]{:S(2)}) collective-permute-start(bf16[8192,128]{1,0:T(8,128)(2,1)S(1)} %get-tuple-element.16), channel_id=1, source_target_pairs={{0,3},{1,0},{2,1},{3,2},{4,7},{5,4},{6,5},{7,6},{8,11},{9,8},{10,9... | collective-permute-start | bytes 6291464 | tf_op jit(solution)/shard_map/ppermute | solution.py:329
  305.4 4.0 copy-start
  306.8 40.1 %all-to-all-start.2 = ((f32[32,24,512]{2,1,0:T(8,128)}), f32[32,24,512]{2,1,0:T(8,128)S(1)}, u32[]{:S(2)}, u32[]{:S(2)}) async-start(f32[32,24,512]{2,1,0:T(8,128)} %broadcast_in_dim.18), calls=%async_computation.2 | async-start | bytes 3145728 | tf_op jit(solution)/shard_map/all_to_all | solution.py:367
  371.1 53.4 %all-to-all-start.4 = ((s16[4,64,8320]{2,1,0:T(8,128)(2,1)}), s16[4,64,8320]{2,1,0:T(8,128)(2,1)}, u32[]{:S(2)}, u32[]{:S(2)}) async-start(s16[4,64,8320]{2,1,0:T(8,128)(2,1)} %update.3), calls=%async_computation.4 | async-start | bytes 8519680 | tf_op jit(solution)/shard_map/all_to_all | solution.py:376
  424.5 52.9 %all-to-all-start.3 = ((s16[4,64,8320]{2,1,0:T(8,128)(2,1)}), s16[4,64,8320]{2,1,0:T(8,128)(2,1)}, u32[]{:S(2)}, u32[]{:S(2)}) async-start(s16[4,64,8320]{2,1,0:T(8,128)(2,1)} %update.2), calls=%async_computation.3 | async-start | bytes 8519680 | tf_op jit(solution)/shard_map/all_to_all | solution.py:376

commit v6 on v5

--- a/solution.py
+++ b/solution.py
@@ -82,7 +82,7 @@
     steps = steps_of(code_ref[:, length:])
     total[...] = jnp.zeros_like(total)
 
-    @pl.loop(0, length // CHUNK)
+    @pl.loop(0, length // CHUNK, unroll=2)
     def _(i):
         value = jnp.concatenate(decoded_chunk(code_ref, steps, i), axis=1)
         high = value.astype(jnp.bfloat16)
@@ -131,7 +131,7 @@
     )
     peaks[...] = jnp.zeros_like(peaks)
 
-    @pl.loop(0, length // CHUNK)
+    @pl.loop(0, length // CHUNK, unroll=2)
     def _(i):
         block = reflector_ref[pl.ds(pl.multiple_of(i * CHUNK, CHUNK), CHUNK), :]
         change = lax.dot_general(
@@ -152,7 +152,7 @@
     out_ref[:, :, length:] = exponent.reshape(split).astype(jnp.int32).astype(jnp.int16)
     inverse = jnp.exp(exponent * (-LN2 / FINE)) * TOP
 
-    @pl.loop(0, length // CHUNK)
+    @pl.loop(0, length // CHUNK, unroll=2)
     def _(i):
         for j in range(CHUNK // GROUP):
             at = lanes(i * CHUNK + j * GROUP)
@@ -237,9 +237,11 @@
         unit = jnp.where(below == 0, 1.0, 0.0)
         block = jnp.where(below > 0, stored, unit).astype(jnp.bfloat16)
         reflector_ref[:, panel * nb : (panel + 1) * nb] = block
-    block = reflector_ref[...]
     product = lax.dot_general(
-        block, block, (((0,), (0,)), ((), ())), preferred_element_type=jnp.float32
+        reflector_ref[:, nb:],
+        reflector_ref[:, :-nb],
+        (((0,), (0,)), ((), ())),
+        preferred_element_type=jnp.float32,
     )
 
     @pl.when(pl.program_id(0) == 0)
@@ -261,11 +263,11 @@
         in_specs=[scalars, scalars] + [pl.BlockSpec((rows, nb), lambda i: (i, 0)) for _ in pieces],
         out_specs=[
             pl.BlockSpec((rows, reach), lambda i: (i, 0)),
-            pl.BlockSpec((reach, reach), lambda i: (0, 0)),
+            pl.BlockSpec((reach - nb, reach - nb), lambda i: (0, 0)),
         ],
         out_shape=[
             jax.ShapeDtypeStruct((length, reach), jnp.bfloat16),
-            jax.ShapeDtypeStruct((reach, reach), jnp.float32),
+            jax.ShapeDtypeStruct((reach - nb, reach - nb), jnp.float32),
         ],
         compiler_params=pltpu.CompilerParams(vmem_limit_bytes=VMEM_LIMIT),
         cost_estimate=pl.CostEstimate(
@@ -336,8 +338,7 @@
     n_col = lax.axis_size("col")
     n_all = lax.axis_size("row") * n_col
     me = lax.axis_index("col")
-    pieces, eigvecs = lax.optimization_barrier((cut_panels(panels[0], n_col), eigvecs))
-    pieces = spread_panels(pieces)
+    pieces = spread_panels(cut_panels(panels[0], n_col))
     triangles = lax.all_gather(tfactors[0], "col")
     triangles = jnp.take(triangles, owners, axis=0)
     code = encode(eigvecs, n_all)
@@ -347,7 +348,7 @@
     length, nb = pieces[0].shape
     first_row = (lax.axis_index("row") * n_col + me) * length
     reflector, gram = reflect(pieces, lax.rem(me - owners + n_col, n_col), offsets - first_row)
-    blocks = [gram[q * nb : (q + 1) * nb, p * nb : (p + 1) * nb] for q, p in PAIRS]
+    blocks = [gram[(q - 1) * nb : q * nb, p * nb : (p + 1) * nb] for q, p in PAIRS]
     blocks += [jnp.zeros_like(blocks[0])] * (-len(blocks) % PANELS)
     packed = [
         jnp.concatenate(blocks[i : i + PANELS], axis=1) for i in range(0, len(blocks), PANELS)

time: 485 us -> 478 us (0.986)
    ppermute x3, waiting for transfers between devices: 188 us -> 183 us  [spread_panels(): lax.ppermute(piece, 'col', [(i, (i + k) % n) for i in range(n)])]
  transfers between devices with their start and end apart: 7 -> 7, of which waited for: 6 -> 5; matrix products, arithmetic and copies ran while one was open for 1% -> 2% of each run, Pallas kernels for 8% -> 8%
where the time goes in v6:
time: 478 us; the launch traced here: 477 us
  waiting for transfers between devices  277 us (58%)
  Pallas kernels  93.5 us (20%)
  blocking collectives  68.1 us (14%)
  starting transfers between devices  23.6 us (5%)
  local copies, waits for them, and re-layouts  11.9 us (2%)
    ppermute x3, waiting for transfers between devices, spread_panels(): lax.ppermute(piece, 'col', [(i, (i + k) % n) for i in range(n)])  183 us
    all_to_all x2, waiting for transfers between devices, local(): part = lax.all_to_all(part, 'col', split_axis=0, concat_axis=0, tiled=True)  74.8 us
    all_to_all x1, blocking collectives, local(): sums = lax.all_to_all(sums, both, split_axis=0, concat_axis=0, tiled=True)  51.2 us
    pallas_call x2, Pallas kernels, update(): pl.pallas_call(update_kernel, grid=(1,), in_specs=[pl.BlockSpec((parts, N...  30.7 us
    all_to_all x1, waiting for transfers between devices, local(): sums = lax.all_to_all(sums, both, split_axis=0, concat_axis=0, tiled=True)  19.2 us
    all_gather x1, blocking collectives, local(): triangles = lax.all_gather(tfactors[0], 'col')  16.9 us
    pallas_call x1, Pallas kernels, project(): pl.pallas_call(project_kernel, grid=(count // rows,), in_specs=[pl.BlockS...  15.9 us
    pallas_call x1, Pallas kernels, reflect(): pl.pallas_call(reflect_kernel, grid=(length // rows,), in_specs=[scalars,...  14.1 us
  transfers between devices with their start and end apart: 7, of which 5 were waited for; matrix products, arithmetic and copies ran while one was open for 2% of the time, Pallas kernels for 8%

profile of v6, /device:TPU:0, one launch (start us, length us, event | category | flops | bytes accessed | tf_op | source)
XLA Modules:
  0.0 476.6 jit_solution(4948282309863025375)
XLA Ops:
  0.0 13.8 %encode.1 = s16[32,16,8320]{2,1,0:T(8,128)(2,1)} custom-call(f32[16,262144]{1,0:T(8,128)} %x_ref.1), custom_call_target="tpu_custom_call" | custom-call | flops 25165824 | bytes 25165824 | tf_op jit(solution)/shard_map/encode/pallas_call | solution.py:55
  13.8 7.4 %all-to-all-start = ((s16[32,16,8320]{2,1,0:T(8,128)(2,1)}), s16[32,16,8320]{2,1,0:T(8,128)(2,1)}, u32[]{:S(2)}, u32[]{:S(2)}) async-start(s16[32,16,8320]{2,1,0:T(8,128)(2,1)} %encode.1), calls=%async_computation | async-start | bytes 17039360 | tf_op jit(solution)/shard_map/all_to_all | solution.py:345
  21.2 0.0 copy-start.1
  21.3 0.0 copy-start.2
  21.3 6.2 %dynamic-slice_bitcast_fusion = (bf16[8192,128]{1,0:T(8,128)(2,1)}, bf16[8192,128]{1,0:T(8,128)(2,1)}, bf16[8192,128]{1,0:T(8,128)(2,1)}, bf16[8192,128]{1,0:T(8,128)(2,1)S(1)}) fusion(bf16[1,32768,128]{2,1,0:T(8,128)(2,1)} %param.6, s32[]{:T(128)S(6)} %select_n.24, s32[]{:T(128)S(6)} %select_n.22, s32[]{:T(128)S(6)} %select_n.21, s32[]{:T(128)S(6)} %select_n.23), kind=kLoop, calls=%fused_computation.1 | loop fusion | bytes 16777232 | tf_op jit(solution)/shard_map/dynamic_slice | solution.py:323
  27.5 2.6 collective-permute-start.2
  30.1 0.0 collective-permute-start
  30.1 1.1 collective-permute-start.1
  31.2 0.0 copy-done.1
  31.2 0.0 copy-done.2
  31.2 0.6 compare_select_fusion
  31.8 126.6 %collective-permute-done.2.refs_3_ = bf16[8192,128]{1,0:T(8,128)(2,1)} collective-permute-done((bf16[8192,128]{1,0:T(8,128)(2,1)}, bf16[8192,128]{1,0:T(8,128)(2,1)}, u32[]{:S(2)}, u32[]{:S(2)}) %collective-permute-start.2) | collective-permute-done | bytes 2097184 | tf_op jit(solution)/shard_map/ppermute | solution.py:331
  158.3 56.1 %collective-permute-done.refs_1_ = bf16[8192,128]{1,0:T(8,128)(2,1)} collective-permute-done((bf16[8192,128]{1,0:T(8,128)(2,1)}, bf16[8192,128]{1,0:T(8,128)(2,1)}, u32[]{:S(2)}, u32[]{:S(2)}) %collective-permute-start) | collective-permute-done | bytes 2097184 | tf_op jit(solution)/shard_map/ppermute | solution.py:331
  214.4 0.0 collective-permute-done.1.refs_2_
  214.4 14.1 %reflect.1 = (bf16[8192,512]{1,0:T(8,128)(2,1)}, f32[384,384]{1,0:T(8,128)}) custom-call(s32[4]{0:T(128)} %get-tuple-element.18.source_ref, s32[4]{0:T(128)} %get-tuple-element.19.shift_ref, bf16[8192,128]{1,0:T(8,128)(2,1)} %get-tuple-element.11.refs_0_, bf16[8192,128]{1,0:T(8,128)(2,1)} %collective-permute-done.refs_1_, ...), custom_call_target="tpu_custom_call" | custom-call | flops 4294967296 | bytes 16777216 | tf_op jit(solution)/shard_map/reflect/pallas_call | solution.py:260
  228.5 0.9 slice.27
  229.4 1.0 fusion.2
  230.4 0.0 all-to-all-done
  230.4 15.9 %project.1 = f32[512,512]{1,0:T(8,128)} custom-call(s16[512,8320]{1,0:T(8,128)(2,1)} %bitcast.1.code_ref, bf16[8192,512]{1,0:T(8,128)(2,1)} %get-tuple-element.7.reflector_ref), custom_call_target="tpu_custom_call" | custom-call | flops 8589934592 | bytes 16908288 | tf_op jit(solution)/shard_map/project/pallas_call | solution.py:101
  246.4 1.4 pad_maximum_fusion
  247.8 51.2 %all_to_all.25 = f32[32,24,512]{2,1,0:T(8,128)S(1)} all-to-all(f32[32,24,512]{2,1,0:T(8,128)S(1)} %pad_maximum_fusion), channel_id=1, replica_groups=mesh['row'=8,'col'=4] {'row','col'}, dimensions={0} | all-to-all | bytes 3145728 | tf_op jit(solution)/shard_map/all_to_all | solution.py:365
  298.9 0.1 reduce_sum.9
  299.0 0.0 copy-start
  299.0 1.3 broadcast_in_dim.18
  300.4 2.7 all-to-all-start.2
  303.1 0.0 copy-done
  303.1 16.9 %all_gather.3 = bf16[4,128,128]{2,1,0:T(8,128)(2,1)S(1)} all-gather(bf16[1,128,128]{2,1,0:T(8,128)(2,1)S(1)} %copy-done), channel_id=1, replica_groups=mesh['row'=8,'col'=4] {'col'}, dimensions={0}, use_global_device_ids=true | all-gather | bytes 163840 | tf_op jit(solution)/shard_map/all_gather | solution.py:342
  320.0 0.6 gather_fusion
  320.6 0.7 broadcast_select_fusion.triangle_ref
  321.4 19.2 %all-to-all-done.2 = f32[32,24,512]{2,1,0:T(8,128)S(1)} async-done(((f32[32,24,512]{2,1,0:T(8,128)}), f32[32,24,512]{2,1,0:T(8,128)S(1)}, u32[]{:S(2)}, u32[]{:S(2)}) %all-to-all-start.2) | async-done | bytes 1572896 | tf_op jit(solution)/shard_map/all_to_all | solution.py:368
  340.5 0.8 slice_bitcast_fusion.gram_ref
  341.4 1.1 slice.32
  342.4 6.2 %solve.1 = bf16[512,1024]{1,0:T(8,128)(2,1)} custom-call(f32[512,512]{1,0:T(8,128)} %bitcast.19, f32[256,512]{1,0:T(8,128)} %slice_bitcast_fusion.gram_ref, bf16[4,128,128]{2,1,0:T(8,128)(2,1)} %broadcast_select_fusion.triangle_ref), custom_call_target="tpu_custom_call" | custom-call | tf_op jit(solution)/shard_map/solve/pallas_call | solution.py:309
  348.6 15.3 %update.3 = s16[4,64,8320]{2,1,0:T(8,128)(2,1)} custom-call(s16[4,2,64,8320]{3,2,1,0:T(8,128)(2,1)} %bitcast.code_ref, bf16[4,2,64,1024]{3,2,1,0:T(8,128)(2,1)} %bitcast.17, bf16[8192,512]{1,0:T(8,128)(2,1)} %get-tuple-element.7.reflector_ref), custom_call_target="tpu_custom_call" | custom-call | flops 4294967296 | bytes 16908288 | tf_op jit(solution)/shard_map/update/pallas_call | solution.py:167
  364.0 4.9 %all-to-all-start.4 = ((s16[4,64,8320]{2,1,0:T(8,128)(2,1)}), s16[4,64,8320]{2,1,0:T(8,128)(2,1)}, u32[]{:S(2)}, u32[]{:S(2)}) async-start(s16[4,64,8320]{2,1,0:T(8,128)(2,1)} %update.3), calls=%async_computation.4 | async-start | bytes 8519680 | tf_op jit(solution)/shard_map/all_to_all | solution.py:377
  368.9 15.3 %update.2 = s16[4,64,8320]{2,1,0:T(8,128)(2,1)} custom-call(s16[4,2,64,8320]{3,2,1,0:T(8,128)(2,1)} %bitcast.code_ref, bf16[4,2,64,1024]{3,2,1,0:T(8,128)(2,1)} %bitcast.18, bf16[8192,512]{1,0:T(8,128)(2,1)} %get-tuple-element.7.reflector_ref), custom_call_target="tpu_custom_call" | custom-call | flops 4294967296 | bytes 16908288 | tf_op jit(solution)/shard_map/update/pallas_call | solution.py:167
  384.2 33.2 %all-to-all-done.4.code_ref = s16[4,64,8320]{2,1,0:T(8,128)(2,1)} async-done(((s16[4,64,8320]{2,1,0:T(8,128)(2,1)}), s16[4,64,8320]{2,1,0:T(8,128)(2,1)}, u32[]{:S(2)}, u32[]{:S(2)}) %all-to-all-start.4) | async-done | bytes 4259872 | tf_op jit(solution)/shard_map/all_to_all | solution.py:377
  417.4 4.9 %all-to-all-start.3 = ((s16[4,64,8320]{2,1,0:T(8,128)(2,1)}), s16[4,64,8320]{2,1,0:T(8,128)(2,1)}, u32[]{:S(2)}, u32[]{:S(2)}) async-start(s16[4,64,8320]{2,1,0:T(8,128)(2,1)} %update.2), calls=%async_computation.3 | async-start | bytes 8519680 | tf_op jit(solution)/shard_map/all_to_all | solution.py:377
  422.2 6.4 %decode.2.refs_0_ = f32[128,32768]{1,0:T(8,128)} custom-call(s16[4,64,8320]{2,1,0:T(8,128)(2,1)} %all-to-all-done.4.code_ref), custom_call_target="tpu_custom_call" | custom-call | flops 4194304 | bytes 12582912 | tf_op jit(solution)/shard_map/decode/pallas_call | solution.py:206
  428.6 41.6 %all-to-all-done.3.code_ref = s16[4,64,8320]{2,1,0:T(8,128)(2,1)} async-done(((s16[4,64,8320]{2,1,0:T(8,128)(2,1)}), s16[4,64,8320]{2,1,0:T(8,128)(2,1)}, u32[]{:S(2)}, u32[]{:S(2)}) %all-to-all-start.3) | async-done | bytes 4259872 | tf_op jit(solution)/shard_map/all_to_all | solution.py:377
  470.2 6.4 %decode.3 = f32[128,32768]{1,0:T(8,128)} custom-call(s16[4,64,8320]{2,1,0:T(8,128)(2,1)} %all-to-all-done.3.code_ref, f32[128,32768]{1,0:T(8,128)} %decode.2.refs_0_), custom_call_target="tpu_custom_call", output_to_operand_aliasing={{}: (1, {})} | custom-call | flops 4194304 | bytes 12582912 | tf_op jit(solution)/shard_map/decode/pallas_call | solution.py:206
  (3 shorter events, 0.1 us)
Async XLA Ops:
  13.8 216.6 %all-to-all-start = ((s16[32,16,8320]{2,1,0:T(8,128)(2,1)}), s16[32,16,8320]{2,1,0:T(8,128)(2,1)}, u32[]{:S(2)}, u32[]{:S(2)}) async-start(s16[32,16,8320]{2,1,0:T(8,128)(2,1)} %encode.1), calls=%async_computation | async-start | bytes 17039360 | tf_op jit(solution)/shard_map/all_to_all | solution.py:345
  21.2 10.0 %copy-start.1 = (s32[4]{0:T(128)S(1)}, s32[4]{0:T(128)}, u32[]{:S(2)}) copy-start(s32[4]{0:T(128)} %param.9) | copy-start | bytes 52
  21.3 9.9 %copy-start.2 = (s32[4]{0:T(128)S(1)}, s32[4]{0:T(128)}, u32[]{:S(2)}) copy-start(s32[4]{0:T(128)} %param.8) | copy-start | bytes 52
  27.5 130.9 %collective-permute-start.2 = (bf16[8192,128]{1,0:T(8,128)(2,1)}, bf16[8192,128]{1,0:T(8,128)(2,1)}, u32[]{:S(2)}, u32[]{:S(2)}) collective-permute-start(bf16[8192,128]{1,0:T(8,128)(2,1)} %get-tuple-element.9), channel_id=1, source_target_pairs={{0,3},{1,0},{2,1},{3,2},{4,7},{5,4},{6,5},{7,6},{8,11},{9,8},{10,9... | collective-permute-start | bytes 6291464 | tf_op jit(solution)/shard_map/ppermute | solution.py:331
  30.1 184.3 %collective-permute-start = (bf16[8192,128]{1,0:T(8,128)(2,1)}, bf16[8192,128]{1,0:T(8,128)(2,1)}, u32[]{:S(2)}, u32[]{:S(2)}) collective-permute-start(bf16[8192,128]{1,0:T(8,128)(2,1)} %get-tuple-element.10), channel_id=1, source_target_pairs={{0,1},{1,2},{2,3},{3,0},{4,5},{5,6},{6,7},{7,4},{8,9},{9,10},{10,1... | collective-permute-start | bytes 6291464 | tf_op jit(solution)/shard_map/ppermute | solution.py:331
  30.1 184.3 %collective-permute-start.1 = (bf16[8192,128]{1,0:T(8,128)(2,1)S(1)}, bf16[8192,128]{1,0:T(8,128)(2,1)}, u32[]{:S(2)}, u32[]{:S(2)}) collective-permute-start(bf16[8192,128]{1,0:T(8,128)(2,1)S(1)} %get-tuple-element.12), channel_id=1, source_target_pairs={{0,2},{1,3},{2,0},{3,1},{4,6},{5,7},{6,4},{7,5},{8,10},{9,11},{10,... | collective-permute-start | bytes 6291464 | tf_op jit(solution)/shard_map/ppermute | solution.py:331
  299.0 4.0 copy-start
  300.4 40.1 %all-to-all-start.2 = ((f32[32,24,512]{2,1,0:T(8,128)}), f32[32,24,512]{2,1,0:T(8,128)S(1)}, u32[]{:S(2)}, u32[]{:S(2)}) async-start(f32[32,24,512]{2,1,0:T(8,128)} %broadcast_in_dim.18), calls=%async_computation.2 | async-start | bytes 3145728 | tf_op jit(solution)/shard_map/all_to_all | solution.py:368
  364.0 53.4 %all-to-all-start.4 = ((s16[4,64,8320]{2,1,0:T(8,128)(2,1)}), s16[4,64,8320]{2,1,0:T(8,128)(2,1)}, u32[]{:S(2)}, u32[]{:S(2)}) async-start(s16[4,64,8320]{2,1,0:T(8,128)(2,1)} %update.3), calls=%async_computation.4 | async-start | bytes 8519680 | tf_op jit(solution)/shard_map/all_to_all | solution.py:377
  417.4 52.9 %all-to-all-start.3 = ((s16[4,64,8320]{2,1,0:T(8,128)(2,1)}), s16[4,64,8320]{2,1,0:T(8,128)(2,1)}, u32[]{:S(2)}, u32[]{:S(2)}) async-start(s16[4,64,8320]{2,1,0:T(8,128)(2,1)} %update.2), calls=%async_computation.3 | async-start | bytes 8519680 | tf_op jit(solution)/shard_map/all_to_all | solution.py:377
